TPU v7x, 32 devices: a whole 2x2x4 slice. The times are simulated.
32 devices in a mesh: ctx: 4 (over y, x), exp: 4 (over z), dp: 2 (over core).
Axes of the slice: x: 2, y: 2, z: 4, core: 2. Of those that a mesh axis runs over, the one named last changes fastest.
Arguments:
- residual: bfloat16 [512, 4096], P('ctx', ('exp', 'dp')), may hold values from -6 to 6
- ssm_values: bfloat16 [512, 4096], P('ctx', ('exp', 'dp')), may hold values from -6 to 6
- ssm_keys: bfloat16 [512, 64], P('ctx'), may hold values from -6 to 6
- ssm_queries: bfloat16 [512, 64], P('ctx'), may hold values from -0.03125 to 0.03125
- log_decay: float32 [512, 64], P('ctx', ('exp', 'dp')), may hold values from -1 to 0, as said below
- expert_ids: int32 [512, 2], P('ctx'), may hold values from 0 to 3, all different within a row; in each aligned block of 128 rows (0 to 127, 128 to 255, ...) at most 80 rows name the same one
- gate_probs: float32 [512, 2], P('ctx'), may hold values from 0.2 to 1
- norm_gain: float32 [4096], P(('exp', 'dp')), may hold values from 0.5 to 1.5
- w_gate: bfloat16 [4, 4096, 8192], P('exp', None, ('ctx', 'dp')), may hold values from -0.09375 to 0.09375
- w_up: bfloat16 [4, 4096, 8192], P('exp', None, ('ctx', 'dp')), may hold values from -0.09375 to 0.09375
- w_down: bfloat16 [4, 4096, 8192], P('exp', None, ('ctx', 'dp')), may hold values from -0.0625 to 0.0625
- out_grad: bfloat16 [512, 4096], P('ctx', ('exp', 'dp')), may hold values from -6 to 6
Outputs:
- grad_residual: bfloat16 [512, 4096], P('ctx', ('exp', 'dp'))
- grad_values: bfloat16 [512, 4096], P('ctx', ('exp', 'dp'))
- grad_keys: float32 [512, 64], P('ctx')
- grad_queries: float32 [512, 64], P('ctx')
- grad_decay: float32 [512, 64], P('ctx', ('exp', 'dp'))
- grad_probs: float32 [512, 2], P('ctx')
- grad_gain: float32 [4096], P(('exp', 'dp'))
- w_gate_grad: bfloat16 [4, 4096, 8192], P('exp', None, ('ctx', 'dp'))
- w_up_grad: bfloat16 [4, 4096, 8192], P('exp', None, ('ctx', 'dp'))
- w_down_grad: bfloat16 [4, 4096, 8192], P('exp', None, ('ctx', 'dp'))
Inputs may be any that keep to these rules, and one draw needn't show every extreme that they name: `expert_ids`: each token names two different experts; among the 128 tokens of one index of ctx (aligned blocks) no expert is named more than 80 times, a bound that some block reaches. `log_decay`: negative everywhere.
All inputs are finite; a program needn't handle non-finite values.
Results may differ from a plain program's by a relative error of at most 0.028.
Values may be sent and summed in bfloat16 or wider, within the bound.
A program may use at most 128 MiB of HBM per device.

v0:
```python
import jax
import jax.numpy as jnp
from jax import lax
from jax.sharding import PartitionSpec as P

HIGH = lax.Precision.HIGHEST
EPS = 1e-05


def entering(x, axis, join, neutral):
    place = lax.axis_index(axis)
    gathered = jax.tree.map(
        lambda a, kind: lax.all_gather(a.astype(kind), axis), x, (jnp.bfloat16, jnp.bfloat16)
    )
    state = jax.tree.map(lambda a, e: jnp.zeros_like(a) + jnp.asarray(e, a.dtype), x, neutral)

    def entering_one(step, state):
        return join(
            state,
            jax.tree.map(
                lambda a, own: lax.dynamic_index_in_dim(a, step, 0, False).astype(own.dtype),
                gathered,
                x,
            ),
        )

    return lax.fori_loop(0, place, entering_one, state)


def carried_in(x, axis, join, neutral):
    count = lax.axis_size(axis)
    place = lax.axis_index(axis)
    ahead = count - 1 - place
    gathered = jax.tree.map(
        lambda a, kind: lax.all_gather(a.astype(kind), axis),
        x,
        jax.tree.map(lambda a: jnp.bfloat16 if a.dtype == jnp.float32 else a.dtype, x),
    )
    state = jax.tree.map(lambda a, e: jnp.zeros_like(a) + jnp.asarray(e, a.dtype), x, neutral)

    def carried_one(step, state):
        source = count - 1 - step
        return join(
            state,
            jax.tree.map(
                lambda a, own: lax.dynamic_index_in_dim(a, source, 0, False).astype(own.dtype),
                gathered,
                x,
            ),
        )

    return lax.fori_loop(0, ahead, carried_one, state)


def block_state(values, key_rows, log_decay):
    cumulative = jnp.cumsum(log_decay, axis=0)
    total_log = cumulative[-1]
    tail_decay = jnp.exp(total_log[None, :] - cumulative)
    weighted = tail_decay[:, :, None] * values
    state_local = jnp.einsum("shp,sn->hpn", weighted, key_rows, precision=HIGH)
    return (jnp.exp(total_log), state_local)


def block_output(values, key_rows, queries, log_decay, state_in):
    cumulative = jnp.cumsum(log_decay, axis=0)
    length = values.shape[0]
    row_index = lax.broadcasted_iota(jnp.int32, (length, length), 0)
    col_index = lax.broadcasted_iota(jnp.int32, (length, length), 1)
    causal = (row_index >= col_index)[None]
    cum_heads = cumulative.T
    log_gap = jnp.where(causal, cum_heads[:, :, None] - cum_heads[:, None, :], 0.0)
    decay_mat = jnp.where(causal, jnp.exp(log_gap), 0.0)
    scores = jnp.dot(queries, key_rows.T, precision=HIGH)
    inner_part = jnp.einsum("hts,shp->thp", decay_mat * scores[None], values, precision=HIGH)
    carried = jnp.einsum("tn,hpn->thp", queries, state_in, precision=HIGH)
    return inner_part + jnp.exp(cumulative)[:, :, None] * carried


def silu_parts(gate_act):
    sigmoid_val = jax.nn.sigmoid(gate_act)
    return (gate_act * sigmoid_val, sigmoid_val * (1.0 + gate_act * (1.0 - sigmoid_val)))


def route_slots(token_ids, expert_count):
    owners = token_ids.reshape(-1)
    onehot = (owners[:, None] == jnp.arange(expert_count, dtype=jnp.int32)[None, :]).astype(
        jnp.int32
    )
    rank_before = jnp.cumsum(onehot, axis=0) - onehot
    return (owners, jnp.sum(rank_before * onehot, axis=1))


def combine_states(earlier_part, later_part):
    return (
        earlier_part[0] * later_part[0],
        later_part[0][:, None, None] * earlier_part[1] + later_part[1],
    )


def arrange_rows(gathered, ctx_count, dp_count):
    capacity = gathered.shape[1]
    exp_count = gathered.shape[2]
    feat = gathered.shape[3]
    shaped = gathered.reshape(ctx_count, dp_count, capacity, exp_count, feat)
    return shaped.transpose(0, 2, 3, 1, 4).reshape(
        ctx_count * capacity, exp_count * dp_count * feat
    )


def arrange_sums(full_term, ctx_count, dp_count, exp_count, capacity):
    feat = full_term.shape[1] // (exp_count * dp_count)
    shaped = full_term.reshape(ctx_count, capacity, exp_count, dp_count, feat)
    return shaped.transpose(0, 3, 1, 2, 4).reshape(
        ctx_count * dp_count * capacity, exp_count * feat
    )


def per_device(
    residual,
    ssm_values,
    ssm_keys,
    ssm_queries,
    log_decay,
    expert_ids,
    gate_probs,
    norm_gain,
    w_gate,
    w_up,
    w_down,
    out_grad,
):
    tokens = residual.shape[0]
    feat = residual.shape[1]
    heads_here = log_decay.shape[1]
    head_size = feat // heads_here
    model_width = w_gate.shape[1]
    ctx_count = lax.axis_size("ctx")
    exp_count = lax.axis_size("exp")
    dp_count = lax.axis_size("dp")
    expert_count = w_gate.shape[0] * exp_count
    capacity = 5 * tokens // (2 * expert_count)
    block_vals = ssm_values.astype(jnp.float32).reshape(tokens, heads_here, head_size)
    block_keys = ssm_keys.astype(jnp.float32)
    block_queries = ssm_queries.astype(jnp.float32)
    (decay_total, state_local), state_pull = jax.vjp(block_state, block_vals, block_keys, log_decay)
    neutral = (jnp.ones_like(decay_total), jnp.zeros_like(state_local))
    state_in = entering((decay_total, state_local), "ctx", combine_states, neutral)[1]
    mixer_out, output_pull = jax.vjp(
        block_output, block_vals, block_keys, block_queries, log_decay, state_in
    )
    hidden = (residual.astype(jnp.float32) + mixer_out.reshape(tokens, feat)).astype(jnp.bfloat16)
    hidden_f = hidden.astype(jnp.float32)
    square_sum = lax.psum(jnp.sum(hidden_f * hidden_f, axis=1), ("exp", "dp"))
    inv_rms = lax.rsqrt(square_sum / model_width + EPS)[:, None]
    normed = (hidden_f * inv_rms * norm_gain[None, :]).astype(jnp.bfloat16)
    owners, slot_index = route_slots(expert_ids, expert_count)
    pair_rows = jnp.repeat(normed, 2, axis=0)
    dout_rows = jnp.repeat(out_grad, 2, axis=0)
    pair_prob = gate_probs.reshape(-1)
    pair_cot = (pair_prob[:, None] * dout_rows.astype(jnp.float32)).astype(jnp.bfloat16)
    empty = jnp.zeros((expert_count, capacity, feat), jnp.bfloat16)
    send_rows = empty.at[owners, slot_index].set(pair_rows).reshape(expert_count, capacity, 1, feat)
    got_rows = lax.all_to_all(send_rows, "exp", split_axis=0, concat_axis=2, tiled=True)
    all_rows = lax.all_gather(got_rows, ("ctx", "dp"), axis=0, tiled=True)
    rows_flat = arrange_rows(all_rows, ctx_count, dp_count)
    act_gate = jnp.dot(rows_flat, w_gate[0], preferred_element_type=jnp.float32)
    act_up = jnp.dot(rows_flat, w_up[0], preferred_element_type=jnp.float32)
    swish_val, swish_slope = silu_parts(act_gate)
    hidden_act = (swish_val * act_up).astype(jnp.bfloat16)
    full_out = lax.dot_general(
        hidden_act, w_down[0], (((1,), (1,)), ((), ())), preferred_element_type=jnp.float32
    )
    out_total = lax.psum_scatter(
        arrange_sums(full_out, ctx_count, dp_count, exp_count, capacity).astype(jnp.bfloat16),
        ("ctx", "dp"),
        scatter_dimension=0,
        tiled=True,
    )
    expert_out = out_total.reshape(1, capacity, exp_count, feat)
    back_out = lax.all_to_all(expert_out, "exp", split_axis=2, concat_axis=0, tiled=True).reshape(
        expert_count, capacity, feat
    )
    out_pairs = back_out[owners, slot_index]
    probs_part = jnp.einsum(
        "kd,kd->k", out_pairs, dout_rows, preferred_element_type=jnp.float32
    ).reshape(tokens, 2)
    grad_probs = lax.psum(probs_part, ("exp", "dp"))
    send_cot = empty.at[owners, slot_index].set(pair_cot).reshape(expert_count, capacity, 1, feat)
    got_cot = lax.all_to_all(send_cot, "exp", split_axis=0, concat_axis=2, tiled=True)
    all_cot = lax.all_gather(got_cot, ("ctx", "dp"), axis=0, tiled=True)
    cot_flat = arrange_rows(all_cot, ctx_count, dp_count)
    grad_act = jnp.dot(cot_flat, w_down[0], preferred_element_type=jnp.float32)
    grad_gate = (grad_act * act_up * swish_slope).astype(jnp.bfloat16)
    grad_up = (grad_act * swish_val).astype(jnp.bfloat16)
    full_back = lax.dot_general(
        grad_gate, w_gate[0], (((1,), (1,)), ((), ())), preferred_element_type=jnp.float32
    ) + lax.dot_general(
        grad_up, w_up[0], (((1,), (1,)), ((), ())), preferred_element_type=jnp.float32
    )
    back_total = lax.psum_scatter(
        arrange_sums(full_back, ctx_count, dp_count, exp_count, capacity).astype(jnp.bfloat16),
        ("ctx", "dp"),
        scatter_dimension=0,
        tiled=True,
    )
    pair_back = back_total.reshape(1, capacity, exp_count, feat)
    back_in = lax.all_to_all(pair_back, "exp", split_axis=2, concat_axis=0, tiled=True).reshape(
        expert_count, capacity, feat
    )
    grad_normed = (
        back_in[owners, slot_index].astype(jnp.float32).reshape(tokens, 2, feat).sum(axis=1)
    )
    w_gate_grad = jnp.dot(rows_flat.T, grad_gate, preferred_element_type=jnp.float32).astype(
        jnp.bfloat16
    )[None]
    w_up_grad = jnp.dot(rows_flat.T, grad_up, preferred_element_type=jnp.float32).astype(
        jnp.bfloat16
    )[None]
    w_down_grad = jnp.dot(cot_flat.T, hidden_act, preferred_element_type=jnp.float32).astype(
        jnp.bfloat16
    )[None]
    scaled = grad_normed * norm_gain[None, :]
    inner_sum = lax.psum(jnp.sum(hidden_f * scaled, axis=1), ("exp", "dp"))
    projection = (inner_sum / model_width)[:, None]
    grad_hidden = (
        out_grad.astype(jnp.float32) + inv_rms * scaled - hidden_f * inv_rms**3 * projection
    )
    gain_part = jnp.sum(grad_normed * hidden_f * inv_rms, axis=0)
    grad_gain = lax.psum(gain_part, "ctx")
    grad_mixer = grad_hidden.reshape(tokens, heads_here, head_size)
    vals_first, keys_first, queries_part, decay_first, carry_cot = output_pull(grad_mixer)
    grad_state = carried_in((decay_total, carry_cot), "ctx", combine_states, neutral)[1]
    grad_total = jnp.sum(grad_state * state_in, axis=(1, 2))
    vals_second, keys_second, decay_second = state_pull((grad_total, grad_state))
    grad_keys, grad_queries = (
        lax.psum((keys_first + keys_second).astype(jnp.bfloat16), ("exp", "dp")).astype(
            jnp.float32
        ),
        lax.psum(queries_part.astype(jnp.bfloat16), ("exp", "dp")).astype(jnp.float32),
    )
    grad_residual = grad_hidden.astype(jnp.bfloat16)
    grad_values = (vals_first + vals_second).reshape(tokens, feat).astype(jnp.bfloat16)
    grad_decay = decay_first + decay_second
    return (
        grad_residual,
        grad_values,
        grad_keys,
        grad_queries,
        grad_decay,
        grad_probs,
        grad_gain,
        w_gate_grad,
        w_up_grad,
        w_down_grad,
    )


def solution(mesh):
    return jax.shard_map(
        per_device,
        mesh=mesh,
        in_specs=(
            P("ctx", ("exp", "dp")),
            P("ctx", ("exp", "dp")),
            P("ctx", None),
            P("ctx", None),
            P("ctx", ("exp", "dp")),
            P("ctx", None),
            P("ctx", None),
            P(("exp", "dp")),
            P("exp", None, ("ctx", "dp")),
            P("exp", None, ("ctx", "dp")),
            P("exp", None, ("ctx", "dp")),
            P("ctx", ("exp", "dp")),
        ),
        out_specs=(
            P("ctx", ("exp", "dp")),
            P("ctx", ("exp", "dp")),
            P("ctx", None),
            P("ctx", None),
            P("ctx", ("exp", "dp")),
            P("ctx", None),
            P(("exp", "dp")),
            P("exp", None, ("ctx", "dp")),
            P("exp", None, ("ctx", "dp")),
            P("exp", None, ("ctx", "dp")),
        ),
        check_vma=False,
    )
```

profile of v0, /device:TPU:0, one launch (start us, length us, event | category | flops | bytes accessed | tf_op | source)
XLA Modules:
  0.0 372.5 jit_solution(743245798410474168)
XLA Ops:
  12.4 13.9 %scatter_fusion = bf16[4,80,512]{2,1,0:T(8,128)(2,1)S(1)} fusion(bf16[4,80,512]{2,1,0:T(8,128)(2,1)S(1)} %broadcast_in_dim.73.clone.1, s32[256]{0:T(256)S(1)} %bitcast.201, bf16[256,512]{1,0:T(8,128)(2,1)S(1)} %fusion.22), kind=kCustom, calls=%fused_computation.2 | custom fusion | bytes 788480 | tf_op jit(solution)/shard_map/scatter | solution.py:188
  26.3 16.5 %all_to_all.66 = bf16[4,80,1,512]{3,1,2,0:T(8,128)(2,1)} all-to-all(bf16[4,80,1,512]{3,1,2,0:T(8,128)(2,1)S(1)} %bitcast.204), channel_id=1, replica_groups=mesh['ctx'=4,'exp'=4,'dp'=2] {'exp'}, dimensions={0} | all-to-all | bytes 655360 | tf_op jit(solution)/shard_map/all_to_all | solution.py:189
  43.2 7.9 %all-gather.4 = bf16[4,1,8]{2,1,0:T(2,128)(2,1)S(1)} all-gather(bf16[1,1,8]{2,1,0:T(2,128)(2,1)S(1)} %get-tuple-element.229), channel_id=1, replica_groups=mesh['ctx'=4,'exp'=4,'dp'=2] {'ctx'}, dimensions={0}, use_global_device_ids=true | all-gather | bytes 80 | tf_op jit(solution)/shard_map/all_gather | solution.py:13
  51.7 10.8 %all-gather = bf16[32,64,64]{2,1,0:T(8,128)(2,1)S(1)} all-gather(bf16[8,64,64]{2,1,0:T(8,128)(2,1)S(1)} %convolution_convert_fusion.1), channel_id=2, replica_groups=mesh['ctx'=4,'exp'=4,'dp'=2] {'ctx'}, dimensions={0}, use_global_device_ids=true | all-gather | bytes 327680 | tf_op jit(solution)/shard_map/all_gather | solution.py:13
  64.1 13.6 %psum.42 = f32[128]{0:T(128)S(1)} all-reduce(f32[128]{0:T(128)S(1)} %get-tuple-element.221), channel_id=1, replica_groups=mesh['ctx'=4,'exp'=4,'dp'=2] {'exp','dp'}, use_global_device_ids=true, to_apply=%region_4.5 | all-reduce | flops 128 | bytes 1024 | tf_op jit(solution)/shard_map/psum | solution.py:153
  78.6 13.9 %scatter_fusion.1 = bf16[4,80,512]{2,1,0:T(8,128)(2,1)S(1)} fusion(bf16[4,80,512]{2,1,0:T(8,128)(2,1)S(1)} %broadcast_in_dim.73.clone, s32[256]{0:T(256)S(1)} %bitcast.202, bf16[256,512]{1,0:T(8,128)(2,1)S(1)} %reshape.273), kind=kCustom, calls=%fused_computation.3 | custom fusion | bytes 788480 | tf_op jit(solution)/shard_map/scatter | solution.py:162
  92.5 13.7 %all_to_all.67 = bf16[4,80,1,512]{3,1,2,0:T(8,128)(2,1)} all-to-all(bf16[4,80,1,512]{3,1,2,0:T(8,128)(2,1)S(1)} %bitcast.203), channel_id=1, replica_groups=mesh['ctx'=4,'exp'=4,'dp'=2] {'exp'}, dimensions={0} | all-to-all | bytes 655360 | tf_op jit(solution)/shard_map/all_to_all | solution.py:163
  106.3 4.4 %copy.130 = bf16[4,80,4,2,512]{4,3,2,1,0:T(2,128)(2,1)S(1)} copy(bf16[4,80,4,2,512]{4,1,2,3,0:T(8,128)(2,1)} %bitcast.217) | data formatting | bytes 5242880 | tf_op jit(solution)/shard_map/transpose | solution.py:105
  110.7 4.1 %reshape.236 = bf16[320,4096]{1,0:T(8,128)(2,1)} reshape(bf16[4,80,4,2,512]{4,3,2,1,0:T(2,128)(2,1)S(1)} %copy.130) | data formatting | bytes 5242880 | tf_op jit(solution)/shard_map/reshape | solution.py:105
  114.8 20.3 %all-gather.10.cloned.1.call-done = bf16[8,80,4,1,512]{4,1,3,2,0:T(8,128)(2,1)} async-done(((bf16[1,80,4,1,512]{4,1,3,2,0:T(8,128)(2,1)}), bf16[8,80,4,1,512]{4,1,3,2,0:T(8,128)(2,1)}) %all-gather.10.cloned.1.call-update) | async-done | bytes 2621456 | tf_op jit(solution)/shard_map/all_gather | solution.py:164
  135.0 4.4 %copy.133 = bf16[4,80,4,2,512]{4,3,2,1,0:T(2,128)(2,1)S(1)} copy(bf16[4,80,4,2,512]{4,1,2,3,0:T(8,128)(2,1)} %bitcast.218) | data formatting | bytes 5242880 | tf_op jit(solution)/shard_map/transpose | solution.py:105
  139.5 3.6 reshape.240
  143.1 6.2 %fusion.2 = f32[320,1024]{1,0:T(8,128)S(1)} fusion(bf16[320,4096]{1,0:T(8,128)(2,1)} %reshape.240, bf16[1,4096,1024]{2,1,0:T(8,128)(2,1)} %param.24), kind=kOutput, calls=%fused_computation.10 | convolution fusion | flops 2684354560 | bytes 12320768 | tf_op jit(solution)/shard_map/dot_general | solution.py:166
  149.4 5.4 %fusion.8 = f32[320,1024]{1,0:T(8,128)S(1)} fusion(bf16[320,4096]{1,0:T(8,128)(2,1)S(1)} %copy-done.3, bf16[1,4096,1024]{2,1,0:T(8,128)(2,1)} %param.26), kind=kOutput, calls=%fused_computation.16 | convolution fusion | flops 2684354560 | bytes 12320768 | tf_op jit(solution)/shard_map/dot_general | solution.py:192
  155.1 3.3 multiply_convert_fusion
  158.5 3.2 convert_bitcast_fusion.3
  163.7 2.4 copy.157
  166.1 5.5 %fusion = f32[320,4096]{1,0:T(8,128)S(1)} fusion(bf16[320,1024]{1,0:T(8,128)(2,1)S(1)} %get-tuple-element.226, bf16[1,4096,1024]{2,1,0:T(8,128)(2,1)} %param.24), kind=kOutput, calls=%fused_computation.8 | convolution fusion | flops 2684354560 | bytes 14286848 | tf_op jit(solution)/shard_map/dot_general | solution.py:195
  171.7 10.9 %fusion.13 = bf16[320,4096]{1,0:T(8,128)(2,1)} fusion(f32[320,4096]{1,0:T(8,128)S(1)} %fusion, bf16[320,1024]{1,0:T(8,128)(2,1)S(1)} %get-tuple-element.227, bf16[1,4096,1024]{2,1,0:T(8,128)(2,1)} %param.25), kind=kOutput, calls=%fused_computation.22 | convolution fusion | flops 2686976000 | bytes 16908288 | tf_op jit(solution)/shard_map/dot_general | solution.py:197
  182.5 4.3 %convert_element_type.165 = bf16[4,80,4,2,512]{4,3,2,1,0:T(2,128)(2,1)S(1)} reshape(bf16[320,4096]{1,0:T(8,128)(2,1)} %fusion.13) | data formatting | bytes 5242880 | tf_op jit(solution)/shard_map/convert_element_type | solution.py:201
  187.9 2.3 copy.156
  190.2 10.0 %convert_bitcast_fusion = bf16[1,4096,1024]{2,1,0:T(8,128)(2,1)} fusion(bf16[320,4096]{1,0:T(8,128)(2,1)} %reshape.236, bf16[320,1024]{1,0:T(8,128)(2,1)} %copy-done.19), kind=kOutput, calls=%fused_computation.18 | convolution fusion | flops 2688548864 | bytes 11665408 | tf_op jit(solution)/shard_map/dot_general | solution.py:219
  200.2 9.7 %reduce-scatter.5.cloned.1.call-done = bf16[80,2048]{1,0:T(8,128)(2,1)} async-done(((bf16[640,2048]{1,0:T(8,128)(2,1)}), bf16[80,2048]{1,0:T(8,128)(2,1)}) %reduce-scatter.5.cloned.1.call-update) | async-done | bytes 327696 | tf_op jit(solution)/shard_map/reduce_scatter | solution.py:173
  211.9 4.8 %all-to-all-start.3 = ((bf16[1,80,4,512]{3,1,0,2:T(8,128)(2,1)}), bf16[1,80,4,512]{3,1,0,2:T(8,128)(2,1)S(1)}, u32[]{:S(2)}, u32[]{:S(2)}) async-start(bf16[1,80,4,512]{3,1,0,2:T(8,128)(2,1)} %copy.142), calls=%async_computation.5 | async-start | bytes 655360 | tf_op jit(solution)/shard_map/all_to_all | solution.py:180
  216.7 7.9 %convert_bitcast_fusion.1 = bf16[1,4096,1024]{2,1,0:T(8,128)(2,1)} fusion(bf16[320,4096]{1,0:T(8,128)(2,1)S(1)} %copy-done.2, bf16[320,1024]{1,0:T(8,128)(2,1)} %copy-done.20), kind=kOutput, calls=%fused_computation.19 | convolution fusion | flops 2688548864 | bytes 11665408 | tf_op jit(solution)/shard_map/dot_general | solution.py:216
  224.7 32.6 %reduce-scatter.3.cloned.1.call-done = bf16[80,2048]{1,0:T(8,128)(2,1)} async-done(((bf16[640,2048]{1,0:T(8,128)(2,1)}), bf16[80,2048]{1,0:T(8,128)(2,1)}) %reduce-scatter.3.cloned.1.call-update) | async-done | bytes 327696 | tf_op jit(solution)/shard_map/reduce_scatter | solution.py:200
  259.3 4.6 %all-to-all-start.2 = ((bf16[1,80,4,512]{3,1,0,2:T(8,128)(2,1)}), bf16[1,80,4,512]{3,1,0,2:T(8,128)(2,1)S(1)}, u32[]{:S(2)}, u32[]{:S(2)}) async-start(bf16[1,80,4,512]{3,1,0,2:T(8,128)(2,1)} %copy.135), calls=%async_computation.3 | async-start | bytes 655360 | tf_op jit(solution)/shard_map/all_to_all | solution.py:207
  263.9 9.8 %convert_bitcast_fusion.2 = bf16[1,4096,1024]{2,1,0:T(8,128)(2,1)} fusion(bf16[320,4096]{1,0:T(8,128)(2,1)} %reshape.240, bf16[320,1024]{1,0:T(8,128)(2,1)} %copy-done.21), kind=kOutput, calls=%fused_computation.20 | convolution fusion | flops 2688548864 | bytes 11665408 | tf_op jit(solution)/shard_map/dot_general | solution.py:213
  279.4 29.7 %all-reduce.1 = (f32[128]{0:T(128)S(1)}, f32[128,2]{1,0:T(8,128)S(1)}) all-reduce(f32[128]{0:T(128)S(1)} %get-tuple-element.194, f32[128,2]{1,0:T(8,128)S(1)} %reshape.247), channel_id=1, replica_groups=mesh['ctx'=4,'exp'=4,'dp'=2] {'exp','dp'}, use_global_device_ids=true, to_apply=%region_13.14 | all-reduce | flops 384 | bytes 3072 | tf_op jit(solution)/shard_map/psum | solution.py:223
  311.0 10.1 %all-gather.3 = bf16[32,64,64]{2,1,0:T(8,128)(2,1)S(1)} all-gather(bf16[8,64,64]{2,1,0:T(8,128)(2,1)S(1)} %convolution_convert_fusion), channel_id=5, replica_groups=mesh['ctx'=4,'exp'=4,'dp'=2] {'ctx'}, dimensions={0}, use_global_device_ids=true | all-gather | bytes 327680 | tf_op jit(solution)/shard_map/all_gather | solution.py:35
  322.6 9.1 %psum.47 = f32[512]{0:T(512)} all-reduce(f32[512]{0:T(512)S(1)} %get-tuple-element.193), channel_id=1, replica_groups=mesh['ctx'=4,'exp'=4,'dp'=2] {'ctx'}, use_global_device_ids=true, to_apply=%region_30.31 | all-reduce | flops 512 | bytes 4096 | tf_op jit(solution)/shard_map/psum | solution.py:229
  335.2 26.0 %all-reduce.2 = (bf16[128,64]{0,1:T(8,128)(2,1)S(1)}, bf16[128,64]{0,1:T(8,128)(2,1)S(1)}) all-reduce(bf16[128,64]{0,1:T(8,128)(2,1)S(1)} %fusion.20, bf16[128,64]{0,1:T(8,128)(2,1)S(1)} %fusion.21), channel_id=1, replica_groups=mesh['ctx'=4,'exp'=4,'dp'=2] {'exp','dp'}, use_global_device_ids=true, to_apply=%region_17.18 | all-reduce | flops 16384 | bytes 65536 | tf_op jit(solution)/shard_map/psum | solution.py:236
  (157 shorter events, 33.2 us)
Async XLA Ops:
  7.2 44.3 %copy-start = (bf16[128,64]{0,1:T(8,128)(2,1)S(1)}, bf16[128,64]{0,1:T(8,128)(2,1)}, u32[]{:S(2)}) copy-start(bf16[128,64]{0,1:T(8,128)(2,1)} %param.18) | copy-start | bytes 49156
  7.2 99.1 %all-gather.8.cloned.1.call-start = ((), (), s32[]{:S(2)}) async-start(), calls=%async_computation.8 | async-start | bytes 2949120 | tf_op jit(solution)/shard_map/all_gather | solution.py:190
  12.2 14.1 %copy-start.4 = (bf16[256,512]{1,0:T(8,128)(2,1)}, bf16[256,512]{1,0:T(8,128)(2,1)S(1)}, u32[]{:S(2)}) copy-start(bf16[256,512]{1,0:T(8,128)(2,1)S(1)} %reshape.233) | copy-start | bytes 786436
  12.4 30.5 %copy-start.15 = (f32[128,8]{0,1:T(8,128)S(1)}, f32[128,8]{0,1:T(8,128)}, u32[]{:S(2)}) copy-start(f32[128,8]{0,1:T(8,128)} %param.20) | copy-start | bytes 12292
  12.4 38.9 %copy-start.13 = (bf16[128,512]{1,0:T(8,128)(2,1)S(1)}, bf16[128,512]{1,0:T(8,128)(2,1)}, u32[]{:S(2)}) copy-start(bf16[128,512]{1,0:T(8,128)(2,1)} %param.17) | copy-start | bytes 393220
  12.4 50.1 %copy-start.11 = (bf16[128,64]{0,1:T(8,128)(2,1)S(1)}, bf16[128,64]{0,1:T(8,128)(2,1)}, u32[]{:S(2)}) copy-start(bf16[128,64]{0,1:T(8,128)(2,1)} %param.19) | copy-start | bytes 49156
  42.8 92.2 %all-gather.10.cloned.1.call-start = ((), (), s32[]{:S(2)}) async-start(), calls=%async_computation.9 | async-start | bytes 2949120 | tf_op jit(solution)/shard_map/all_gather | solution.py:164
  51.4 11.6 %copy-start.6 = (bf16[128,512]{0,1:T(8,128)(2,1)}, bf16[128,512]{0,1:T(8,128)(2,1)S(1)}, u32[]{:S(2)}) copy-start(bf16[128,512]{0,1:T(8,128)(2,1)S(1)} %copy.119) | copy-start | bytes 393220
  62.7 1.3 copy-start.12
  62.7 15.5 %copy-start.14 = (f32[512]{0:T(512)S(1)}, f32[512]{0:T(512)}, u32[]{:S(2)}) copy-start(f32[512]{0:T(512)} %param.23) | copy-start | bytes 6148
  62.8 1.3 copy-start.16
  63.1 0.8 copy-start.8
  106.2 103.7 %reduce-scatter.5.cloned.1.call-start = ((), (), s32[]{:S(2)}) async-start(), calls=%async_computation.7 | async-start | bytes 2949120 | tf_op jit(solution)/shard_map/reduce_scatter | solution.py:173
  143.1 6.2 %copy-start.3 = (bf16[320,4096]{1,0:T(8,128)(2,1)S(1)}, bf16[320,4096]{1,0:T(8,128)(2,1)}, u32[]{:S(2)}) copy-start(bf16[320,4096]{1,0:T(8,128)(2,1)} %reshape.236) | copy-start | bytes 7864324
  143.1 11.7 %slice-start.2 = ((s8[8388608]{0:T(1024)(128)(4,1)}), s8[4194304]{0:T(1024)(128)(4,1)S(1)}, s32[]{:S(2)}) async-start(s8[8388608]{0:T(1024)(128)(4,1)} %bitcast.234), calls=%async_computation.12 | async-start | bytes 8388608
  143.1 15.4 %slice-start = ((s8[8388608]{0:T(1024)(128)(4,1)}), s8[4194304]{0:T(1024)(128)(4,1)S(1)}, s32[]{:S(2)}) async-start(s8[8388608]{0:T(1024)(128)(4,1)} %bitcast.231), calls=%async_computation.10 | async-start | bytes 8388608
  149.3 5.5 %copy-start.1 = (bf16[320,4096]{1,0:T(8,128)(2,1)S(1)}, bf16[320,4096]{1,0:T(8,128)(2,1)}, u32[]{:S(2)}) copy-start(bf16[320,4096]{1,0:T(8,128)(2,1)} %reshape.240) | copy-start | bytes 7864324
  149.3 5.8 %slice-start.3 = ((s8[8388608]{0:T(1024)(128)(4,1)}), s8[4194304]{0:T(1024)(128)(4,1)S(1)}, s32[]{:S(2)}) async-start(s8[8388608]{0:T(1024)(128)(4,1)} %bitcast.234), calls=%async_computation.13 | async-start | bytes 8388608
  149.4 9.1 %slice-start.1 = ((s8[8388608]{0:T(1024)(128)(4,1)}), s8[4194304]{0:T(1024)(128)(4,1)S(1)}, s32[]{:S(2)}) async-start(s8[8388608]{0:T(1024)(128)(4,1)} %bitcast.231), calls=%async_computation.11 | async-start | bytes 8388608
  158.4 3.2 copy-start.19
  158.4 7.7 %copy-start.21 = (bf16[320,1024]{1,0:T(8,128)(2,1)}, bf16[320,1024]{1,0:T(8,128)(2,1)S(1)}, u32[]{:S(2)}) copy-start(bf16[320,1024]{1,0:T(8,128)(2,1)S(1)} %get-tuple-element.226) | copy-start | bytes 1966084
  158.5 13.2 %copy-start.20 = (bf16[320,1024]{1,0:T(8,128)(2,1)}, bf16[320,1024]{1,0:T(8,128)(2,1)S(1)}, u32[]{:S(2)}) copy-start(bf16[320,1024]{1,0:T(8,128)(2,1)S(1)} %get-tuple-element.227) | copy-start | bytes 1966084
  166.1 91.2 %reduce-scatter.3.cloned.1.call-start = ((), (), s32[]{:S(2)}) async-start(), calls=%async_computation.6 | async-start | bytes 2949120 | tf_op jit(solution)/shard_map/reduce_scatter | solution.py:200
  190.2 26.5 %copy-start.2 = (bf16[320,4096]{1,0:T(8,128)(2,1)S(1)}, bf16[320,4096]{1,0:T(8,128)(2,1)}, u32[]{:S(2)}) copy-start(bf16[320,4096]{1,0:T(8,128)(2,1)} %reshape.240) | copy-start | bytes 7864324
  211.9 47.4 %all-to-all-start.3 = ((bf16[1,80,4,512]{3,1,0,2:T(8,128)(2,1)}), bf16[1,80,4,512]{3,1,0,2:T(8,128)(2,1)S(1)}, u32[]{:S(2)}, u32[]{:S(2)}) async-start(bf16[1,80,4,512]{3,1,0,2:T(8,128)(2,1)} %copy.142), calls=%async_computation.5 | async-start | bytes 655360 | tf_op jit(solution)/shard_map/all_to_all | solution.py:180
  259.3 16.9 %all-to-all-start.2 = ((bf16[1,80,4,512]{3,1,0,2:T(8,128)(2,1)}), bf16[1,80,4,512]{3,1,0,2:T(8,128)(2,1)S(1)}, u32[]{:S(2)}, u32[]{:S(2)}) async-start(bf16[1,80,4,512]{3,1,0,2:T(8,128)(2,1)} %copy.135), calls=%async_computation.3 | async-start | bytes 655360 | tf_op jit(solution)/shard_map/all_to_all | solution.py:207
  273.7 2.1 copy-start.5
  275.8 33.3 %copy-start.10 = (bf16[128,512]{1,0:T(8,128)(2,1)S(1)}, bf16[128,512]{1,0:T(8,128)(2,1)}, u32[]{:S(2)}) copy-start(bf16[128,512]{1,0:T(8,128)(2,1)} %param.27) | copy-start | bytes 393220
  275.9 33.3 %copy-start.18 = (f32[128]{0:T(128)S(1)}, f32[128]{0:T(128)}, u32[]{:S(2)}) copy-start(f32[128]{0:T(128)} %get-tuple-element.230) | copy-start | bytes 1540
  276.2 33.9 %copy-start.9 = (f32[128,8,64]{0,2,1:T(8,128)S(1)}, f32[128,8,64]{0,2,1:T(8,128)}, u32[]{:S(2)}) copy-start(f32[128,8,64]{0,2,1:T(8,128)} %copy-done.8) | copy-start | bytes 786436
  278.6 42.5 %copy-start.17 = (bf16[4,8]{1,0:T(4,128)(2,1)S(1)}, bf16[4,8]{1,0:T(4,128)(2,1)}, u32[]{:S(2)}) copy-start(bf16[4,8]{1,0:T(4,128)(2,1)} %copy-done.16) | copy-start | bytes 196
  310.8 11.0 %copy-start.7 = (bf16[128,512]{0,1:T(8,128)(2,1)S(1)}, bf16[128,512]{0,1:T(8,128)(2,1)}, u32[]{:S(2)}) copy-start(bf16[128,512]{0,1:T(8,128)(2,1)} %copy-done.6) | copy-start | bytes 393220
Sparse Core Ops, SparseCore 0:
  42.9 31.3 all-gather.7
  106.3 28.6 all-gather.9
  166.2 43.6 reduce-scatter.4
  213.6 43.6 reduce-scatter.2
where the time goes:
time: 379 us; the launch traced here: 372 us
  blocking collectives  137 us (36%)
  local copies, waits for them, and re-layouts  72.2 us (19%)
  matrix products  67.3 us (18%)
  waiting for transfers between devices  62.7 us (17%)
  between operations  15 us (4%)
  starting transfers between devices  9.59 us (3%)
  other arithmetic  8.36 us (2%)
    reduce_scatter x1, waiting for transfers between devices, per_device(): lax.psum_scatter(arrange_sums(full_back, ctx_count, dp_count, exp_count,...  32.6 us
    psum x1, blocking collectives, per_device(): inner_sum = lax.psum(jnp.sum(hidden_f * scaled, axis=1), ('exp', 'dp'))  29.7 us
    psum x1, blocking collectives, per_device(): lax.psum((keys_first + keys_second).astype(jnp.bfloat16), ('exp', 'dp'))  26 us
    all_gather x1, waiting for transfers between devices, per_device(): all_rows = lax.all_gather(got_rows, ('ctx', 'dp'), axis=0, tiled=True)  20.3 us
    all_gather x2, blocking collectives, entering(): lax.all_gather(a.astype(kind), axis)  18.7 us
    all_to_all x1, blocking collectives, per_device(): lax.all_to_all(send_cot, 'exp', split_axis=0, concat_axis=2, tiled=True)  16.5 us
    scatter x1, local copies, waits for them, and re-layouts, per_device(): empty.at[owners, slot_index].set(pair_cot)  13.9 us
    scatter x1, local copies, waits for them, and re-layouts, per_device(): empty.at[owners, slot_index].set(pair_rows)  13.9 us
  transfers between devices with their start and end apart: 6, of which 3 were waited for; matrix products, arithmetic and copies ran while one was open for 22% of the time, Pallas kernels for 0%

commit v1 on v0

--- a/solution.py
+++ b/solution.py
@@ -52,8 +52,16 @@
     return lax.fori_loop(0, ahead, carried_one, state)
 
 
+def running_sum(x):
+    length = x.shape[0]
+    row_index = lax.broadcasted_iota(jnp.int32, (length, length), 0)
+    col_index = lax.broadcasted_iota(jnp.int32, (length, length), 1)
+    lower = (row_index >= col_index).astype(jnp.float32)
+    return jnp.dot(lower, x, precision=HIGH)
+
+
 def block_state(values, key_rows, log_decay):
-    cumulative = jnp.cumsum(log_decay, axis=0)
+    cumulative = running_sum(log_decay)
     total_log = cumulative[-1]
     tail_decay = jnp.exp(total_log[None, :] - cumulative)
     weighted = tail_decay[:, :, None] * values
@@ -62,7 +70,7 @@
 
 
 def block_output(values, key_rows, queries, log_decay, state_in):
-    cumulative = jnp.cumsum(log_decay, axis=0)
+    cumulative = running_sum(log_decay)
     length = values.shape[0]
     row_index = lax.broadcasted_iota(jnp.int32, (length, length), 0)
     col_index = lax.broadcasted_iota(jnp.int32, (length, length), 1)
@@ -86,7 +94,7 @@
     onehot = (owners[:, None] == jnp.arange(expert_count, dtype=jnp.int32)[None, :]).astype(
         jnp.int32
     )
-    rank_before = jnp.cumsum(onehot, axis=0) - onehot
+    rank_before = running_sum(onehot.astype(jnp.float32)).astype(jnp.int32) - onehot
     return (owners, jnp.sum(rank_before * onehot, axis=1))
 
 

time: 379 us -> 375 us (0.989)
  other arithmetic: 8.36 us -> 4.45 us
    unnamed x62 -> x58, local copies, waits for them, and re-layouts: 9.04 us -> 8.24 us
  transfers between devices with their start and end apart: 6 -> 6, of which waited for: 3 -> 3; matrix products, arithmetic and copies ran while one was open for 22% -> 23% of each run, Pallas kernels for 0% -> 0%
where the time goes in v1:
time: 375 us; the launch traced here: 368 us
  blocking collectives  137 us (37%)
  local copies, waits for them, and re-layouts  70.8 us (19%)
  matrix products  69.1 us (18%)
  waiting for transfers between devices  62.5 us (17%)
  between operations  14.7 us (4%)
  starting transfers between devices  9.52 us (3%)
  other arithmetic  4.45 us (1%)
    reduce_scatter x1, waiting for transfers between devices, per_device(): lax.psum_scatter(arrange_sums(full_back, ctx_count, dp_count, exp_count,...  32.7 us
    psum x1, blocking collectives, per_device(): inner_sum = lax.psum(jnp.sum(hidden_f * scaled, axis=1), ('exp', 'dp'))  29.6 us
    psum x1, blocking collectives, per_device(): lax.psum((keys_first + keys_second).astype(jnp.bfloat16), ('exp', 'dp'))  26 us
    all_gather x1, waiting for transfers between devices, per_device(): all_rows = lax.all_gather(got_rows, ('ctx', 'dp'), axis=0, tiled=True)  20.4 us
    all_gather x2, blocking collectives, entering(): lax.all_gather(a.astype(kind), axis)  18.7 us
    all_to_all x1, blocking collectives, per_device(): lax.all_to_all(send_cot, 'exp', split_axis=0, concat_axis=2, tiled=True)  16.5 us
    scatter x1, local copies, waits for them, and re-layouts, per_device(): empty.at[owners, slot_index].set(pair_cot)  13.9 us
    scatter x1, local copies, waits for them, and re-layouts, per_device(): empty.at[owners, slot_index].set(pair_rows)  13.9 us
  transfers between devices with their start and end apart: 6, of which 3 were waited for; matrix products, arithmetic and copies ran while one was open for 23% of the time, Pallas kernels for 0%

profile of v1, /device:TPU:0, one launch (start us, length us, event | category | flops | bytes accessed | tf_op | source)
XLA Modules:
  0.0 368.4 jit_solution(16279228184612114886)
XLA Ops:
  10.9 13.9 %scatter_fusion = bf16[4,80,512]{2,1,0:T(8,128)(2,1)S(1)} fusion(bf16[4,80,512]{2,1,0:T(8,128)(2,1)S(1)} %broadcast_in_dim.73.clone.1, s32[256]{0:T(256)S(1)} %bitcast.177, bf16[256,512]{1,0:T(8,128)(2,1)S(1)} %fusion.25), kind=kCustom, calls=%fused_computation.2 | custom fusion | bytes 788480 | tf_op jit(solution)/shard_map/scatter | solution.py:196
  24.8 16.5 %all_to_all.66 = bf16[4,80,1,512]{3,1,2,0:T(8,128)(2,1)} all-to-all(bf16[4,80,1,512]{3,1,2,0:T(8,128)(2,1)S(1)} %bitcast.180), channel_id=1, replica_groups=mesh['ctx'=4,'exp'=4,'dp'=2] {'exp'}, dimensions={0} | all-to-all | bytes 655360 | tf_op jit(solution)/shard_map/all_to_all | solution.py:197
  41.7 7.9 %all-gather.4 = bf16[4,1,8]{2,1,0:T(2,128)(2,1)S(1)} all-gather(bf16[1,1,8]{2,1,0:T(2,128)(2,1)S(1)} %bitcast.207), channel_id=1, replica_groups=mesh['ctx'=4,'exp'=4,'dp'=2] {'ctx'}, dimensions={0}, use_global_device_ids=true | all-gather | bytes 80 | tf_op jit(solution)/shard_map/all_gather | solution.py:13
  50.3 10.8 %all-gather = bf16[32,64,64]{2,1,0:T(8,128)(2,1)S(1)} all-gather(bf16[8,64,64]{2,1,0:T(8,128)(2,1)S(1)} %convolution_convert_fusion.1), channel_id=2, replica_groups=mesh['ctx'=4,'exp'=4,'dp'=2] {'ctx'}, dimensions={0}, use_global_device_ids=true | all-gather | bytes 327680 | tf_op jit(solution)/shard_map/all_gather | solution.py:13
  62.7 13.6 %psum.42 = f32[128]{0:T(128)S(1)} all-reduce(f32[128]{0:T(128)S(1)} %get-tuple-element.211), channel_id=1, replica_groups=mesh['ctx'=4,'exp'=4,'dp'=2] {'exp','dp'}, use_global_device_ids=true, to_apply=%region_3.4 | all-reduce | flops 128 | bytes 1024 | tf_op jit(solution)/shard_map/psum | solution.py:161
  76.8 13.9 %scatter_fusion.1 = bf16[4,80,512]{2,1,0:T(8,128)(2,1)S(1)} fusion(bf16[4,80,512]{2,1,0:T(8,128)(2,1)S(1)} %broadcast_in_dim.73.clone, s32[256]{0:T(256)S(1)} %bitcast.178, bf16[256,512]{1,0:T(8,128)(2,1)S(1)} %reshape.238), kind=kCustom, calls=%fused_computation.3 | custom fusion | bytes 788480 | tf_op jit(solution)/shard_map/scatter | solution.py:170
  90.6 13.7 %all_to_all.67 = bf16[4,80,1,512]{3,1,2,0:T(8,128)(2,1)} all-to-all(bf16[4,80,1,512]{3,1,2,0:T(8,128)(2,1)S(1)} %bitcast.179), channel_id=1, replica_groups=mesh['ctx'=4,'exp'=4,'dp'=2] {'exp'}, dimensions={0} | all-to-all | bytes 655360 | tf_op jit(solution)/shard_map/all_to_all | solution.py:171
  104.4 4.4 %copy.70 = bf16[4,80,4,2,512]{4,3,2,1,0:T(2,128)(2,1)S(1)} copy(bf16[4,80,4,2,512]{4,1,2,3,0:T(8,128)(2,1)} %bitcast.193) | data formatting | bytes 5242880 | tf_op jit(solution)/shard_map/transpose | solution.py:113
  108.8 3.9 %reshape.201 = bf16[320,4096]{1,0:T(8,128)(2,1)} reshape(bf16[4,80,4,2,512]{4,3,2,1,0:T(2,128)(2,1)S(1)} %copy.70) | data formatting | bytes 5242880 | tf_op jit(solution)/shard_map/reshape | solution.py:113
  112.7 20.4 %all-gather.10.cloned.1.call-done = bf16[8,80,4,1,512]{4,1,3,2,0:T(8,128)(2,1)} async-done(((bf16[1,80,4,1,512]{4,1,3,2,0:T(8,128)(2,1)}), bf16[8,80,4,1,512]{4,1,3,2,0:T(8,128)(2,1)}) %all-gather.10.cloned.1.call-update) | async-done | bytes 2621456 | tf_op jit(solution)/shard_map/all_gather | solution.py:172
  133.2 4.4 %copy.73 = bf16[4,80,4,2,512]{4,3,2,1,0:T(2,128)(2,1)S(1)} copy(bf16[4,80,4,2,512]{4,1,2,3,0:T(8,128)(2,1)} %bitcast.194) | data formatting | bytes 5242880 | tf_op jit(solution)/shard_map/transpose | solution.py:113
  137.6 3.6 reshape.205
  141.2 6.2 %fusion.2 = f32[320,1024]{1,0:T(8,128)S(1)} fusion(bf16[320,4096]{1,0:T(8,128)(2,1)} %reshape.205, bf16[1,4096,1024]{2,1,0:T(8,128)(2,1)} %param.24), kind=kOutput, calls=%fused_computation.10 | convolution fusion | flops 2684354560 | bytes 12320768 | tf_op jit(solution)/shard_map/dot_general | solution.py:174
  147.5 5.4 %fusion.8 = f32[320,1024]{1,0:T(8,128)S(1)} fusion(bf16[320,4096]{1,0:T(8,128)(2,1)S(1)} %copy-done.3, bf16[1,4096,1024]{2,1,0:T(8,128)(2,1)} %param.26), kind=kOutput, calls=%fused_computation.16 | convolution fusion | flops 2684354560 | bytes 12320768 | tf_op jit(solution)/shard_map/dot_general | solution.py:200
  153.3 3.3 multiply_convert_fusion
  156.6 3.2 convert_bitcast_fusion.3
  161.8 2.4 copy.95
  164.3 5.9 %fusion = f32[320,4096]{1,0:T(8,128)S(1)} fusion(bf16[320,1024]{1,0:T(8,128)(2,1)S(1)} %get-tuple-element.216, bf16[1,4096,1024]{2,1,0:T(8,128)(2,1)} %param.24), kind=kOutput, calls=%fused_computation.8 | convolution fusion | flops 2684354560 | bytes 14286848 | tf_op jit(solution)/shard_map/dot_general | solution.py:203
  170.2 10.9 %fusion.13 = bf16[320,4096]{1,0:T(8,128)(2,1)} fusion(f32[320,4096]{1,0:T(8,128)S(1)} %fusion, bf16[320,1024]{1,0:T(8,128)(2,1)S(1)} %get-tuple-element.217, bf16[1,4096,1024]{2,1,0:T(8,128)(2,1)} %param.25), kind=kOutput, calls=%fused_computation.22 | convolution fusion | flops 2686976000 | bytes 16908288 | tf_op jit(solution)/shard_map/dot_general | solution.py:205
  181.1 4.3 %convert_element_type.171 = bf16[4,80,4,2,512]{4,3,2,1,0:T(2,128)(2,1)S(1)} reshape(bf16[320,4096]{1,0:T(8,128)(2,1)} %fusion.13) | data formatting | bytes 5242880 | tf_op jit(solution)/shard_map/convert_element_type | solution.py:209
  186.4 2.3 copy.94
  188.8 10.0 %convert_bitcast_fusion = bf16[1,4096,1024]{2,1,0:T(8,128)(2,1)} fusion(bf16[320,4096]{1,0:T(8,128)(2,1)} %reshape.201, bf16[320,1024]{1,0:T(8,128)(2,1)} %copy-done.18), kind=kOutput, calls=%fused_computation.18 | convolution fusion | flops 2688548864 | bytes 11665408 | tf_op jit(solution)/shard_map/dot_general | solution.py:227
  198.8 9.3 %reduce-scatter.5.cloned.1.call-done = bf16[80,2048]{1,0:T(8,128)(2,1)} async-done(((bf16[640,2048]{1,0:T(8,128)(2,1)}), bf16[80,2048]{1,0:T(8,128)(2,1)}) %reduce-scatter.5.cloned.1.call-update) | async-done | bytes 327696 | tf_op jit(solution)/shard_map/reduce_scatter | solution.py:181
  210.0 4.8 %all-to-all-start.3 = ((bf16[1,80,4,512]{3,1,0,2:T(8,128)(2,1)}), bf16[1,80,4,512]{3,1,0,2:T(8,128)(2,1)S(1)}, u32[]{:S(2)}, u32[]{:S(2)}) async-start(bf16[1,80,4,512]{3,1,0,2:T(8,128)(2,1)} %copy.82), calls=%async_computation.5 | async-start | bytes 655360 | tf_op jit(solution)/shard_map/all_to_all | solution.py:188
  214.8 7.9 %convert_bitcast_fusion.1 = bf16[1,4096,1024]{2,1,0:T(8,128)(2,1)} fusion(bf16[320,4096]{1,0:T(8,128)(2,1)S(1)} %copy-done.2, bf16[320,1024]{1,0:T(8,128)(2,1)} %copy-done.19), kind=kOutput, calls=%fused_computation.19 | convolution fusion | flops 2688548864 | bytes 11665408 | tf_op jit(solution)/shard_map/dot_general | solution.py:224
  222.8 32.7 %reduce-scatter.3.cloned.1.call-done = bf16[80,2048]{1,0:T(8,128)(2,1)} async-done(((bf16[640,2048]{1,0:T(8,128)(2,1)}), bf16[80,2048]{1,0:T(8,128)(2,1)}) %reduce-scatter.3.cloned.1.call-update) | async-done | bytes 327696 | tf_op jit(solution)/shard_map/reduce_scatter | solution.py:208
  257.4 4.6 %all-to-all-start.2 = ((bf16[1,80,4,512]{3,1,0,2:T(8,128)(2,1)}), bf16[1,80,4,512]{3,1,0,2:T(8,128)(2,1)S(1)}, u32[]{:S(2)}, u32[]{:S(2)}) async-start(bf16[1,80,4,512]{3,1,0,2:T(8,128)(2,1)} %copy.75), calls=%async_computation.3 | async-start | bytes 655360 | tf_op jit(solution)/shard_map/all_to_all | solution.py:215
  262.0 9.8 %convert_bitcast_fusion.2 = bf16[1,4096,1024]{2,1,0:T(8,128)(2,1)} fusion(bf16[320,4096]{1,0:T(8,128)(2,1)} %reshape.205, bf16[320,1024]{1,0:T(8,128)(2,1)} %copy-done.20), kind=kOutput, calls=%fused_computation.20 | convolution fusion | flops 2688548864 | bytes 11665408 | tf_op jit(solution)/shard_map/dot_general | solution.py:221
  277.6 29.6 %all-reduce.1 = (f32[128]{0:T(128)S(1)}, f32[128,2]{1,0:T(8,128)S(1)}) all-reduce(f32[128]{0:T(128)S(1)} %get-tuple-element.184, f32[128,2]{1,0:T(8,128)S(1)} %reshape.212), channel_id=1, replica_groups=mesh['ctx'=4,'exp'=4,'dp'=2] {'exp','dp'}, use_global_device_ids=true, to_apply=%region_10.11 | all-reduce | flops 384 | bytes 3072 | tf_op jit(solution)/shard_map/psum | solution.py:231
  309.1 10.1 %all-gather.3 = bf16[32,64,64]{2,1,0:T(8,128)(2,1)S(1)} all-gather(bf16[8,64,64]{2,1,0:T(8,128)(2,1)S(1)} %convolution_convert_fusion), channel_id=5, replica_groups=mesh['ctx'=4,'exp'=4,'dp'=2] {'ctx'}, dimensions={0}, use_global_device_ids=true | all-gather | bytes 327680 | tf_op jit(solution)/shard_map/all_gather | solution.py:35
  320.7 9.0 %psum.47 = f32[512]{0:T(512)} all-reduce(f32[512]{0:T(512)S(1)} %get-tuple-element.183), channel_id=1, replica_groups=mesh['ctx'=4,'exp'=4,'dp'=2] {'ctx'}, use_global_device_ids=true, to_apply=%region_25.26 | all-reduce | flops 512 | bytes 4096 | tf_op jit(solution)/shard_map/psum | solution.py:237
  333.4 26.0 %all-reduce.2 = (bf16[128,64]{0,1:T(8,128)(2,1)S(1)}, bf16[128,64]{0,1:T(8,128)(2,1)S(1)}) all-reduce(bf16[128,64]{0,1:T(8,128)(2,1)S(1)} %fusion.20, bf16[128,64]{0,1:T(8,128)(2,1)S(1)} %fusion.21), channel_id=1, replica_groups=mesh['ctx'=4,'exp'=4,'dp'=2] {'exp','dp'}, use_global_device_ids=true, to_apply=%region_14.15 | all-reduce | flops 16384 | bytes 65536 | tf_op jit(solution)/shard_map/psum | solution.py:244
  (138 shorter events, 29.4 us)
Async XLA Ops:
  7.2 42.9 %copy-start = (bf16[128,64]{0,1:T(8,128)(2,1)S(1)}, bf16[128,64]{0,1:T(8,128)(2,1)}, u32[]{:S(2)}) copy-start(bf16[128,64]{0,1:T(8,128)(2,1)} %param.18) | copy-start | bytes 49156
  7.2 97.2 %all-gather.8.cloned.1.call-start = ((), (), s32[]{:S(2)}) async-start(), calls=%async_computation.8 | async-start | bytes 2949120 | tf_op jit(solution)/shard_map/all_gather | solution.py:198
  10.8 30.5 %copy-start.17 = (f32[128,8]{0,1:T(8,128)S(1)}, f32[128,8]{0,1:T(8,128)}, u32[]{:S(2)}) copy-start(f32[128,8]{0,1:T(8,128)} %param.20) | copy-start | bytes 12292
  10.8 38.8 %copy-start.13 = (bf16[128,512]{1,0:T(8,128)(2,1)S(1)}, bf16[128,512]{1,0:T(8,128)(2,1)}, u32[]{:S(2)}) copy-start(bf16[128,512]{1,0:T(8,128)(2,1)} %param.17) | copy-start | bytes 393220
  10.9 50.3 %copy-start.11 = (bf16[128,64]{0,1:T(8,128)(2,1)S(1)}, bf16[128,64]{0,1:T(8,128)(2,1)}, u32[]{:S(2)}) copy-start(bf16[128,64]{0,1:T(8,128)(2,1)} %param.19) | copy-start | bytes 49156
  41.3 91.9 %all-gather.10.cloned.1.call-start = ((), (), s32[]{:S(2)}) async-start(), calls=%async_computation.9 | async-start | bytes 2949120 | tf_op jit(solution)/shard_map/all_gather | solution.py:172
  49.8 11.9 %copy-start.6 = (bf16[128,512]{0,1:T(8,128)(2,1)}, bf16[128,512]{0,1:T(8,128)(2,1)S(1)}, u32[]{:S(2)}) copy-start(bf16[128,512]{0,1:T(8,128)(2,1)S(1)} %copy.64) | copy-start | bytes 393220
  61.3 1.1 copy-start.14
  61.4 1.3 copy-start.12
  61.4 15.0 %copy-start.16 = (f32[512]{0:T(512)S(1)}, f32[512]{0:T(512)}, u32[]{:S(2)}) copy-start(f32[512]{0:T(512)} %param.23) | copy-start | bytes 6148
  61.7 0.8 copy-start.8
  62.7 13.9 %copy-start.4 = (bf16[128,512]{1,0:T(8,128)(2,1)}, bf16[128,512]{1,0:T(8,128)(2,1)S(1)}, u32[]{:S(2)}) copy-start(bf16[128,512]{1,0:T(8,128)(2,1)S(1)} %get-tuple-element.212) | copy-start | bytes 393220
  104.3 103.7 %reduce-scatter.5.cloned.1.call-start = ((), (), s32[]{:S(2)}) async-start(), calls=%async_computation.7 | async-start | bytes 2949120 | tf_op jit(solution)/shard_map/reduce_scatter | solution.py:181
  141.2 6.2 %copy-start.3 = (bf16[320,4096]{1,0:T(8,128)(2,1)S(1)}, bf16[320,4096]{1,0:T(8,128)(2,1)}, u32[]{:S(2)}) copy-start(bf16[320,4096]{1,0:T(8,128)(2,1)} %reshape.201) | copy-start | bytes 7864324
  141.2 11.7 %slice-start.2 = ((s8[8388608]{0:T(1024)(128)(4,1)}), s8[4194304]{0:T(1024)(128)(4,1)S(1)}, s32[]{:S(2)}) async-start(s8[8388608]{0:T(1024)(128)(4,1)} %bitcast.214), calls=%async_computation.12 | async-start | bytes 8388608
  141.2 15.4 %slice-start = ((s8[8388608]{0:T(1024)(128)(4,1)}), s8[4194304]{0:T(1024)(128)(4,1)S(1)}, s32[]{:S(2)}) async-start(s8[8388608]{0:T(1024)(128)(4,1)} %bitcast.211), calls=%async_computation.10 | async-start | bytes 8388608
  147.5 5.5 %copy-start.1 = (bf16[320,4096]{1,0:T(8,128)(2,1)S(1)}, bf16[320,4096]{1,0:T(8,128)(2,1)}, u32[]{:S(2)}) copy-start(bf16[320,4096]{1,0:T(8,128)(2,1)} %reshape.205) | copy-start | bytes 7864324
  147.5 5.8 %slice-start.3 = ((s8[8388608]{0:T(1024)(128)(4,1)}), s8[4194304]{0:T(1024)(128)(4,1)S(1)}, s32[]{:S(2)}) async-start(s8[8388608]{0:T(1024)(128)(4,1)} %bitcast.214), calls=%async_computation.13 | async-start | bytes 8388608
  147.5 9.1 %slice-start.1 = ((s8[8388608]{0:T(1024)(128)(4,1)}), s8[4194304]{0:T(1024)(128)(4,1)S(1)}, s32[]{:S(2)}) async-start(s8[8388608]{0:T(1024)(128)(4,1)} %bitcast.211), calls=%async_computation.11 | async-start | bytes 8388608
  156.6 3.2 copy-start.18
  156.6 7.7 %copy-start.20 = (bf16[320,1024]{1,0:T(8,128)(2,1)}, bf16[320,1024]{1,0:T(8,128)(2,1)S(1)}, u32[]{:S(2)}) copy-start(bf16[320,1024]{1,0:T(8,128)(2,1)S(1)} %get-tuple-element.216) | copy-start | bytes 1966084
  156.6 13.6 %copy-start.19 = (bf16[320,1024]{1,0:T(8,128)(2,1)}, bf16[320,1024]{1,0:T(8,128)(2,1)S(1)}, u32[]{:S(2)}) copy-start(bf16[320,1024]{1,0:T(8,128)(2,1)S(1)} %get-tuple-element.217) | copy-start | bytes 1966084
  164.2 91.3 %reduce-scatter.3.cloned.1.call-start = ((), (), s32[]{:S(2)}) async-start(), calls=%async_computation.6 | async-start | bytes 2949120 | tf_op jit(solution)/shard_map/reduce_scatter | solution.py:208
  188.8 26.1 %copy-start.2 = (bf16[320,4096]{1,0:T(8,128)(2,1)S(1)}, bf16[320,4096]{1,0:T(8,128)(2,1)}, u32[]{:S(2)}) copy-start(bf16[320,4096]{1,0:T(8,128)(2,1)} %reshape.205) | copy-start | bytes 7864324
  210.0 47.4 %all-to-all-start.3 = ((bf16[1,80,4,512]{3,1,0,2:T(8,128)(2,1)}), bf16[1,80,4,512]{3,1,0,2:T(8,128)(2,1)S(1)}, u32[]{:S(2)}, u32[]{:S(2)}) async-start(bf16[1,80,4,512]{3,1,0,2:T(8,128)(2,1)} %copy.82), calls=%async_computation.5 | async-start | bytes 655360 | tf_op jit(solution)/shard_map/all_to_all | solution.py:188
  257.4 16.8 %all-to-all-start.2 = ((bf16[1,80,4,512]{3,1,0,2:T(8,128)(2,1)}), bf16[1,80,4,512]{3,1,0,2:T(8,128)(2,1)S(1)}, u32[]{:S(2)}, u32[]{:S(2)}) async-start(bf16[1,80,4,512]{3,1,0,2:T(8,128)(2,1)} %copy.75), calls=%async_computation.3 | async-start | bytes 655360 | tf_op jit(solution)/shard_map/all_to_all | solution.py:215
  274.0 3.4 copy-start.5
  274.0 33.2 %copy-start.10 = (bf16[128,512]{1,0:T(8,128)(2,1)S(1)}, bf16[128,512]{1,0:T(8,128)(2,1)}, u32[]{:S(2)}) copy-start(bf16[128,512]{1,0:T(8,128)(2,1)} %param.27) | copy-start | bytes 393220
  274.3 33.9 %copy-start.9 = (f32[128,8,64]{0,2,1:T(8,128)S(1)}, f32[128,8,64]{0,2,1:T(8,128)}, u32[]{:S(2)}) copy-start(f32[128,8,64]{0,2,1:T(8,128)} %copy-done.8) | copy-start | bytes 786436
  308.8 11.0 %copy-start.7 = (bf16[128,512]{0,1:T(8,128)(2,1)S(1)}, bf16[128,512]{0,1:T(8,128)(2,1)}, u32[]{:S(2)}) copy-start(bf16[128,512]{0,1:T(8,128)(2,1)} %copy-done.6) | copy-start | bytes 393220
  319.2 11.2 %copy-start.15 = (f32[128,128]{1,0:T(8,128)S(1)}, f32[128,128]{1,0:T(8,128)}, u32[]{:S(2)}) copy-start(f32[128,128]{1,0:T(8,128)} %copy-done.14) | copy-start | bytes 196612
Sparse Core Ops, SparseCore 0:
  41.4 31.3 all-gather.7
  104.5 28.6 all-gather.9
  164.3 43.6 reduce-scatter.4
  211.8 43.6 reduce-scatter.2

commit v2 on v1

v2 whole, which is shorter than its diff:
```python
import jax
import jax.numpy as jnp
from jax import lax
from jax.sharding import PartitionSpec as P

HIGH = lax.Precision.HIGHEST
EPS = 1e-05


def pass_along(gathered, decays, forward):
    count = lax.axis_size("ctx")
    place = lax.axis_index("ctx")
    state = jnp.zeros(gathered.shape[1:], jnp.float32)
    for step in range(count - 1):
        source = step if forward else count - 1 - step
        joined = decays[source][:, None, None] * state + gathered[source].astype(jnp.float32)
        state = jnp.where(source < place if forward else source > place, joined, state)
    return state


def two_parts(x):
    high = lax.reduce_precision(x, 8, 7)
    return (high.astype(jnp.bfloat16), (x - high).astype(jnp.bfloat16))


def sum_over(x, axes):
    return jnp.sum(lax.all_gather(x, axes).astype(jnp.float32), axis=0)


def running_sum(x):
    length = x.shape[0]
    row_index = lax.broadcasted_iota(jnp.int32, (length, length), 0)
    col_index = lax.broadcasted_iota(jnp.int32, (length, length), 1)
    lower = (row_index >= col_index).astype(jnp.float32)
    return jnp.dot(lower, x, precision=HIGH)


def block_state(values, key_rows, log_decay):
    cumulative = running_sum(log_decay)
    total_log = cumulative[-1]
    tail_decay = jnp.exp(total_log[None, :] - cumulative)
    weighted = tail_decay[:, :, None] * values
    state_local = jnp.einsum("shp,sn->hpn", weighted, key_rows, precision=HIGH)
    return (jnp.exp(total_log), state_local)


def block_output(values, key_rows, queries, log_decay, state_in):
    cumulative = running_sum(log_decay)
    length = values.shape[0]
    row_index = lax.broadcasted_iota(jnp.int32, (length, length), 0)
    col_index = lax.broadcasted_iota(jnp.int32, (length, length), 1)
    causal = (row_index >= col_index)[None]
    cum_heads = cumulative.T
    log_gap = jnp.where(causal, cum_heads[:, :, None] - cum_heads[:, None, :], 0.0)
    decay_mat = jnp.where(causal, jnp.exp(log_gap), 0.0)
    scores = jnp.dot(queries, key_rows.T, precision=HIGH)
    inner_part = jnp.einsum("hts,shp->thp", decay_mat * scores[None], values, precision=HIGH)
    carried = jnp.einsum("tn,hpn->thp", queries, state_in, precision=HIGH)
    return inner_part + jnp.exp(cumulative)[:, :, None] * carried


def silu_parts(gate_act):
    sigmoid_val = jax.nn.sigmoid(gate_act)
    return (gate_act * sigmoid_val, sigmoid_val * (1.0 + gate_act * (1.0 - sigmoid_val)))


def route_slots(token_ids, expert_count):
    owners = token_ids.reshape(-1)
    onehot = (owners[:, None] == jnp.arange(expert_count, dtype=jnp.int32)[None, :]).astype(
        jnp.int32
    )
    rank_before = running_sum(onehot.astype(jnp.float32)).astype(jnp.int32) - onehot
    return (owners, jnp.sum(rank_before * onehot, axis=1))


def arrange_rows(gathered, ctx_count, dp_count):
    exp_count, capacity, feat = gathered.shape[1:]
    shaped = gathered.reshape(ctx_count, dp_count, exp_count, capacity, feat)
    return shaped.transpose(0, 3, 2, 1, 4).reshape(
        ctx_count * capacity, exp_count * dp_count * feat
    )


def arrange_sums(full_term, ctx_count, dp_count, exp_count, capacity):
    feat = full_term.shape[1] // (exp_count * dp_count)
    shaped = full_term.reshape(ctx_count, capacity, exp_count, dp_count, feat)
    return shaped.transpose(0, 3, 2, 1, 4).reshape(-1, feat)


def expert_rows(rows, expert_count, ctx_count, dp_count):
    send = rows.reshape(expert_count, -1, rows.shape[1])
    got = lax.all_to_all(send, "exp", split_axis=0, concat_axis=0, tiled=True)
    return arrange_rows(lax.all_gather(got, ("ctx", "dp")), ctx_count, dp_count)


def token_rows(full_term, ctx_count, dp_count, exp_count, capacity):
    total = lax.psum_scatter(
        arrange_sums(full_term, ctx_count, dp_count, exp_count, capacity),
        ("ctx", "dp"),
        scatter_dimension=0,
        tiled=True,
    )
    feat = total.shape[1]
    back = lax.all_to_all(
        total.reshape(exp_count, capacity, feat), "exp", split_axis=0, concat_axis=0, tiled=True
    )
    return back.reshape(-1, feat)


def rows_back(select, rows):
    return lax.dot_general(
        select, rows, (((0,), (0,)), ((), ())), preferred_element_type=jnp.float32
    )


def per_device(
    residual,
    ssm_values,
    ssm_keys,
    ssm_queries,
    log_decay,
    expert_ids,
    gate_probs,
    norm_gain,
    w_gate,
    w_up,
    w_down,
    out_grad,
):
    tokens = residual.shape[0]
    feat = residual.shape[1]
    heads_here = log_decay.shape[1]
    head_size = feat // heads_here
    model_width = w_gate.shape[1]
    ctx_count = lax.axis_size("ctx")
    exp_count = lax.axis_size("exp")
    dp_count = lax.axis_size("dp")
    expert_count = w_gate.shape[0] * exp_count
    capacity = 5 * tokens // (2 * expert_count)
    block_vals = ssm_values.astype(jnp.float32).reshape(tokens, heads_here, head_size)
    block_keys = ssm_keys.astype(jnp.float32)
    block_queries = ssm_queries.astype(jnp.float32)
    (decay_total, state_local), state_pull = jax.vjp(block_state, block_vals, block_keys, log_decay)
    decay_row = jnp.broadcast_to(decay_total[:, None, None], state_local[:, :1].shape)
    spans = lax.all_gather(
        jnp.concatenate([state_local, decay_row], axis=1).astype(jnp.bfloat16), "ctx"
    )
    decays = spans[:, :, -1, 0].astype(jnp.float32)
    state_in = pass_along(spans[:, :, :-1], decays, True)
    mixer_out, output_pull = jax.vjp(
        block_output, block_vals, block_keys, block_queries, log_decay, state_in
    )
    hidden = (residual.astype(jnp.float32) + mixer_out.reshape(tokens, feat)).astype(jnp.bfloat16)
    hidden_f = hidden.astype(jnp.float32)
    square_sum = sum_over(jnp.sum(hidden_f * hidden_f, axis=1), ("exp", "dp"))
    inv_rms = lax.rsqrt(square_sum / model_width + EPS)[:, None]
    normed = (hidden_f * inv_rms * norm_gain[None, :]).astype(jnp.bfloat16)
    owners, slot_index = route_slots(expert_ids, expert_count)
    row_of = (owners * capacity + slot_index).reshape(tokens, 2)
    row_number = lax.broadcasted_iota(jnp.int32, (expert_count * capacity, tokens), 0)
    first = row_number == row_of[:, 0][None, :]
    second = row_number == row_of[:, 1][None, :]
    select = (first | second).astype(jnp.bfloat16)
    row_prob = jnp.sum(
        jnp.where(first, gate_probs[:, 0][None, :], 0.0)
        + jnp.where(second, gate_probs[:, 1][None, :], 0.0),
        axis=1,
    )
    cot_rows = jnp.dot(select, out_grad, preferred_element_type=jnp.float32)
    cot_rows = (row_prob[:, None] * cot_rows).astype(jnp.bfloat16)
    cot_flat = expert_rows(cot_rows, expert_count, ctx_count, dp_count)
    send_rows = jnp.dot(select, normed, preferred_element_type=jnp.float32).astype(jnp.bfloat16)
    rows_flat = expert_rows(send_rows, expert_count, ctx_count, dp_count)
    act_gate = jnp.dot(rows_flat, w_gate[0], preferred_element_type=jnp.float32)
    act_up = jnp.dot(rows_flat, w_up[0], preferred_element_type=jnp.float32)
    swish_val, swish_slope = silu_parts(act_gate)
    hidden_act = (swish_val * act_up).astype(jnp.bfloat16)
    grad_act = jnp.dot(cot_flat, w_down[0], preferred_element_type=jnp.float32)
    grad_gate = (grad_act * act_up * swish_slope).astype(jnp.bfloat16)
    grad_up = (grad_act * swish_val).astype(jnp.bfloat16)
    full_back = lax.dot_general(
        grad_gate, w_gate[0], (((1,), (1,)), ((), ())), preferred_element_type=jnp.float32
    ) + lax.dot_general(
        grad_up, w_up[0], (((1,), (1,)), ((), ())), preferred_element_type=jnp.float32
    )
    full_back, later_act = lax.optimization_barrier((full_back.astype(jnp.bfloat16), hidden_act))
    back_in = token_rows(full_back, ctx_count, dp_count, exp_count, capacity)
    full_out = lax.dot_general(
        later_act, w_down[0], (((1,), (1,)), ((), ())), preferred_element_type=jnp.float32
    )
    back_out = token_rows(full_out.astype(jnp.bfloat16), ctx_count, dp_count, exp_count, capacity)
    grad_normed = rows_back(select, back_in)
    out_f = out_grad.astype(jnp.float32)
    probs_part = jnp.stack(
        [
            jnp.sum(rows_back(first.astype(jnp.bfloat16), back_out) * out_f, axis=1),
            jnp.sum(rows_back(second.astype(jnp.bfloat16), back_out) * out_f, axis=1),
        ]
    )
    w_gate_grad = jnp.dot(rows_flat.T, grad_gate, preferred_element_type=jnp.float32).astype(
        jnp.bfloat16
    )[None]
    w_up_grad = jnp.dot(rows_flat.T, grad_up, preferred_element_type=jnp.float32).astype(
        jnp.bfloat16
    )[None]
    w_down_grad = jnp.dot(cot_flat.T, hidden_act, preferred_element_type=jnp.float32).astype(
        jnp.bfloat16
    )[None]
    scaled = grad_normed * norm_gain[None, :]
    inner_sum = sum_over(jnp.sum(hidden_f * scaled, axis=1), ("exp", "dp"))
    projection = (inner_sum / model_width)[:, None]
    grad_hidden = (
        out_grad.astype(jnp.float32) + inv_rms * scaled - hidden_f * inv_rms**3 * projection
    )
    gain_part = jnp.sum(grad_normed * hidden_f * inv_rms, axis=0)
    grad_mixer = grad_hidden.reshape(tokens, heads_here, head_size)
    vals_first, keys_first, queries_part, decay_first, carry_cot = output_pull(grad_mixer)
    width = state_local.shape[2]
    gain_rows = [p.reshape(heads_here, -1, width) for p in two_parts(gain_part)]
    carries = lax.all_gather(
        jnp.concatenate([carry_cot.astype(jnp.bfloat16)] + gain_rows, axis=1), "ctx"
    )
    grad_state = pass_along(carries[:, :, :head_size], decays, False)
    gain_high, gain_low = jnp.split(
        jnp.sum(carries[:, :, head_size:].astype(jnp.float32), axis=0), 2, axis=1
    )
    grad_gain = (gain_high + gain_low).reshape(feat)
    grad_total = jnp.sum(grad_state * state_in, axis=(1, 2))
    vals_second, keys_second, decay_second = state_pull((grad_total, grad_state))
    both = jnp.concatenate([keys_first + keys_second, queries_part], axis=1).astype(jnp.bfloat16)
    probs_rows = jnp.concatenate(two_parts(probs_part)).reshape(-1, both.shape[1])
    summed = sum_over(jnp.concatenate([both, probs_rows]), ("exp", "dp"))
    grad_keys, grad_queries = summed[:tokens, :width], summed[:tokens, width:]
    probs_high, probs_low = jnp.split(summed[tokens:].reshape(4, tokens), 2)
    grad_probs = (probs_high + probs_low).T
    grad_residual = grad_hidden.astype(jnp.bfloat16)
    grad_values = (vals_first + vals_second).reshape(tokens, feat).astype(jnp.bfloat16)
    grad_decay = decay_first + decay_second
    return (
        grad_residual,
        grad_values,
        grad_keys,
        grad_queries,
        grad_decay,
        grad_probs,
        grad_gain,
        w_gate_grad,
        w_up_grad,
        w_down_grad,
    )


def solution(mesh):
    return jax.shard_map(
        per_device,
        mesh=mesh,
        in_specs=(
            P("ctx", ("exp", "dp")),
            P("ctx", ("exp", "dp")),
            P("ctx", None),
            P("ctx", None),
            P("ctx", ("exp", "dp")),
            P("ctx", None),
            P("ctx", None),
            P(("exp", "dp")),
            P("exp", None, ("ctx", "dp")),
            P("exp", None, ("ctx", "dp")),
            P("exp", None, ("ctx", "dp")),
            P("ctx", ("exp", "dp")),
        ),
        out_specs=(
            P("ctx", ("exp", "dp")),
            P("ctx", ("exp", "dp")),
            P("ctx", None),
            P("ctx", None),
            P("ctx", ("exp", "dp")),
            P("ctx", None),
            P(("exp", "dp")),
            P("exp", None, ("ctx", "dp")),
            P("exp", None, ("ctx", "dp")),
            P("exp", None, ("ctx", "dp")),
        ),
        check_vma=False,
    )
```

time: 375 us -> 299 us (0.80)
  blocking collectives: 137 us -> 89.8 us
  local copies, waits for them, and re-layouts: 70.8 us -> 40.6 us
    psum x4 -> x0, blocking collectives: 78.3 us -> none  [the longest x1 29.6 us: per_device(): inner_sum = lax.psum(jnp.sum(hidden_f * scaled, axis=1), ('exp', 'dp'))]
    all_gather x3 -> x5, blocking collectives: 28.8 us -> 59.2 us  [the longest x3 36.8 us: sum_over(): return jnp.sum(lax.all_gather(x, axes).astype(jnp.float32), axis=0)]
    scatter x2 -> x0, local copies, waits for them, and re-layouts: 27.7 us -> none  [the longest x1 13.9 us: per_device(): empty.at[owners, slot_index].set(pair_cot)]
    dot_general x1 -> x6, matrix products: 3.15 us -> 13.8 us  [the longest x1 10.3 us: per_device(): lax.dot_general(later_act, w_down[0], (((1,), (1,)), ((), ())), preferred...]
    reshape x10 -> x7, local copies, waits for them, and re-layouts: 12 us -> 21.7 us  [the longest x4 13.7 us: arrange_sums(): shaped = full_term.reshape(ctx_count, capacity, exp_count, dp_count, feat)]
    convert_element_type x4, local copies, waits for them, and re-layouts: 7.68 us -> 0.6 us  [two_parts(): return (high.astype(jnp.bfloat16), (x - high).astype(jnp.bfloat16))]
    dot_general x1, matrix products: 10.9 us -> 4.22 us  [per_device(): lax.dot_general(grad_up, w_up[0], (((1,), (1,)), ((), ())), preferred_ele...]
    gather x2 -> x0, local copies, waits for them, and re-layouts: 4.19 us -> none  [the longest x1 2.1 us: per_device(): back_in[owners, slot_index].astype(jnp.float32).reshape(tokens, 2, feat)]
  transfers between devices with their start and end apart: 6 -> 6, of which waited for: 3 -> 3; matrix products, arithmetic and copies ran while one was open for 23% -> 22% of each run, Pallas kernels for 0% -> 0%
where the time goes in v2:
time: 299 us; the launch traced here: 293 us
  blocking collectives  89.8 us (30%)
  matrix products  69.9 us (23%)
  waiting for transfers between devices  61.7 us (21%)
  local copies, waits for them, and re-layouts  40.6 us (14%)
  between operations  15 us (5%)
  starting transfers between devices  9.62 us (3%)
  other arithmetic  6.66 us (2%)
    reduce_scatter x2, waiting for transfers between devices, token_rows(): lax.psum_scatter(arrange_sums(full_term, ctx_count, dp_count, exp_count,...  41 us
    all_gather x3, blocking collectives, sum_over(): return jnp.sum(lax.all_gather(x, axes).astype(jnp.float32), axis=0)  36.8 us
    all_to_all x2, blocking collectives, expert_rows(): got = lax.all_to_all(send, 'exp', split_axis=0, concat_axis=0, tiled=True)  30.6 us
    all_gather x2, waiting for transfers between devices, expert_rows(): return arrange_rows(lax.all_gather(got, ('ctx', 'dp')), ctx_count, dp_count)  20.7 us
    reshape x4, local copies, waits for them, and re-layouts, arrange_sums(): shaped = full_term.reshape(ctx_count, capacity, exp_count, dp_count, feat)  13.7 us
    all_gather x1, blocking collectives, per_device(): lax.all_gather(jnp.concatenate([state_local, decay_row], axis=1).astype(j...  12.1 us
    dot_general x1, matrix products, per_device(): jnp.dot(cot_flat.T, hidden_act, preferred_element_type=jnp.float32)  10.3 us
    dot_general x1, matrix products, per_device(): lax.dot_general(later_act, w_down[0], (((1,), (1,)), ((), ())), preferred...  10.3 us
  transfers between devices with their start and end apart: 6, of which 3 were waited for; matrix products, arithmetic and copies ran while one was open for 22% of the time, Pallas kernels for 0%

profile of v2, /device:TPU:0, one launch (start us, length us, event | category | flops | bytes accessed | tf_op | source)
XLA Modules:
  0.0 293.2 jit_solution(16480538929786972463)
XLA Ops:
  10.3 1.1 fusion.22
  11.4 16.5 %all_to_all.20 = bf16[4,80,512]{2,1,0:T(8,128)(2,1)} all-to-all(bf16[4,80,512]{2,1,0:T(8,128)(2,1)S(1)} %bitcast.242), channel_id=1, replica_groups=mesh['ctx'=4,'exp'=4,'dp'=2] {'exp'}, dimensions={0} | all-to-all | bytes 655360 | tf_op jit(solution)/shard_map/all_to_all | solution.py:92
  31.0 12.1 %all_gather.40 = bf16[4,8,65,64]{2,3,1,0:T(8,128)(2,1)S(1)} all-gather(bf16[1,8,65,64]{2,3,1,0:T(8,128)(2,1)S(1)} %pad_maximum_fusion), channel_id=1, replica_groups=mesh['ctx'=4,'exp'=4,'dp'=2] {'ctx'}, dimensions={0}, use_global_device_ids=true | all-gather | bytes 332800 | tf_op jit(solution)/shard_map/all_gather | solution.py:145
  45.7 10.3 %all-gather.6 = f32[8,1,128]{2,1,0:T(1,128)S(1)} all-gather(f32[1,1,128]{2,1,0:T(1,128)S(1)} %bitcast.259), channel_id=2, replica_groups=mesh['ctx'=4,'exp'=4,'dp'=2] {'exp','dp'}, dimensions={0}, use_global_device_ids=true | all-gather | bytes 4608 | tf_op jit(solution)/shard_map/all_gather | solution.py:27
  56.9 14.1 %all_to_all.21 = bf16[4,80,512]{2,1,0:T(8,128)(2,1)} all-to-all(bf16[4,80,512]{2,1,0:T(8,128)(2,1)S(1)} %bitcast.243), channel_id=1, replica_groups=mesh['ctx'=4,'exp'=4,'dp'=2] {'exp'}, dimensions={0} | all-to-all | bytes 655360 | tf_op jit(solution)/shard_map/all_to_all | solution.py:92
  71.2 4.4 %copy.167 = bf16[4,80,4,2,512]{4,3,2,1,0:T(2,128)(2,1)S(1)} copy(bf16[4,80,4,2,512]{4,1,2,3,0:T(8,128)(2,1)} %bitcast.237) | data formatting | bytes 5242880 | tf_op jit(solution)/shard_map/transpose | solution.py:79
  75.6 3.8 %reshape.240 = bf16[320,4096]{1,0:T(8,128)(2,1)} reshape(bf16[4,80,4,2,512]{4,3,2,1,0:T(2,128)(2,1)S(1)} %copy.167) | data formatting | bytes 5242880 | tf_op jit(solution)/shard_map/reshape | solution.py:79
  79.4 20.6 %all-gather.14.cloned.1.call-done = bf16[32,80,512]{2,1,0:T(8,128)(2,1)} async-done(((bf16[4,80,512]{2,1,0:T(8,128)(2,1)}), bf16[32,80,512]{2,1,0:T(8,128)(2,1)}) %all-gather.14.cloned.1.call-update) | async-done | bytes 2621456 | tf_op jit(solution)/shard_map/all_gather | solution.py:93
  100.0 4.4 %copy.168 = bf16[4,80,4,2,512]{4,3,2,1,0:T(2,128)(2,1)S(1)} copy(bf16[4,80,4,2,512]{4,1,2,3,0:T(8,128)(2,1)} %bitcast.238) | data formatting | bytes 5242880 | tf_op jit(solution)/shard_map/transpose | solution.py:79
  104.4 3.6 %reshape.243 = bf16[320,4096]{1,0:T(8,128)(2,1)} reshape(bf16[4,80,4,2,512]{4,3,2,1,0:T(2,128)(2,1)S(1)} %copy.168) | data formatting | bytes 5242880 | tf_op jit(solution)/shard_map/reshape | solution.py:79
  108.0 6.2 %fusion.2 = f32[320,1024]{1,0:T(8,128)S(1)} fusion(bf16[320,4096]{1,0:T(8,128)(2,1)} %reshape.243, bf16[1,4096,1024]{2,1,0:T(8,128)(2,1)} %param.20), kind=kOutput, calls=%fused_computation.2 | convolution fusion | flops 2684354560 | bytes 12320768 | tf_op jit(solution)/shard_map/dot_general | solution.py:174
  114.3 5.5 %fusion.10 = f32[320,1024]{1,0:T(8,128)S(1)} fusion(bf16[320,4096]{1,0:T(8,128)(2,1)S(1)} %copy-done.3, bf16[1,4096,1024]{2,1,0:T(8,128)(2,1)} %param.22), kind=kOutput, calls=%fused_computation.10 | convolution fusion | flops 2684354560 | bytes 12320768 | tf_op jit(solution)/shard_map/dot_general | solution.py:178
  120.1 4.2 %multiply_convert_fusion = (bf16[320,1024]{1,0:T(8,128)(2,1)}, bf16[320,1024]{1,0:T(8,128)(2,1)S(1)}, bf16[320,1024]{1,0:T(8,128)(2,1)S(1)}) fusion(f32[320,1024]{1,0:T(8,128)S(1)} %fusion.2, f32[320,1024]{1,0:T(8,128)S(1)} %fusion.10, bf16[320,4096]{1,0:T(8,128)(2,1)S(1)} %copy-done.1, bf16[1,4096,1024]{2,1,0:T(8,128)(2,1)S(1)} %bitcast.268), kind=kOutput, calls=%fused_computation.18 | convolution fusion | flops 2689269760 | bytes 15597568 | tf_op jit(solution)/shard_map/dot_general | solution.py:175
  124.3 2.9 fusion
  127.2 4.2 %fusion.15 = bf16[320,4096]{1,0:T(8,128)(2,1)} fusion(f32[320,4096]{1,0:T(8,128)S(1)} %fusion, bf16[320,1024]{1,0:T(8,128)(2,1)S(1)} %get-tuple-element.99, bf16[1,4096,1024]{2,1,0:T(8,128)(2,1)S(1)} %bitcast.268), kind=kOutput, calls=%fused_computation.16 | convolution fusion | flops 2686976000 | bytes 16908288 | tf_op jit(solution)/shard_map/dot_general | solution.py:183
  131.4 4.5 %reshape.244 = bf16[4,80,4,2,512]{4,3,2,1,0:T(2,128)(2,1)S(1)} reshape(bf16[320,4096]{1,0:T(8,128)(2,1)} %fusion.15) | data formatting | bytes 5242880 | tf_op jit(solution)/shard_map/reshape | solution.py:86
  135.9 2.4 copy.169
  139.5 10.3 %fusion.18 = bf16[320,4096]{1,0:T(8,128)(2,1)} fusion(bf16[320,1024]{1,0:T(8,128)(2,1)S(1)} %copy-done.36, bf16[1,4096,1024]{2,1,0:T(8,128)(2,1)} %param.22), kind=kOutput, calls=%fused_computation.17 | convolution fusion | flops 2685665280 | bytes 11665408 | tf_op jit(solution)/shard_map/dot_general | solution.py:188
  149.7 4.3 %reshape.249 = bf16[4,80,4,2,512]{4,3,2,1,0:T(2,128)(2,1)S(1)} reshape(bf16[320,4096]{1,0:T(8,128)(2,1)} %fusion.18) | data formatting | bytes 5242880 | tf_op jit(solution)/shard_map/reshape | solution.py:86
  154.1 2.4 copy.176
  158.1 10.3 %convert_bitcast_fusion = bf16[1,4096,1024]{2,1,0:T(8,128)(2,1)} fusion(bf16[320,4096]{1,0:T(8,128)(2,1)} %reshape.240, bf16[320,1024]{1,0:T(8,128)(2,1)} %get-tuple-element.13), kind=kOutput, calls=%fused_computation.12 | convolution fusion | flops 2688548864 | bytes 11665408 | tf_op jit(solution)/shard_map/dot_general | solution.py:206
  168.4 6.8 %convert_bitcast_fusion.1 = bf16[1,4096,1024]{2,1,0:T(8,128)(2,1)} fusion(bf16[320,4096]{1,0:T(8,128)(2,1)S(1)} %copy-done.2, bf16[320,1024]{1,0:T(8,128)(2,1)S(1)} %copy-done.35), kind=kOutput, calls=%fused_computation.13 | convolution fusion | flops 2688548864 | bytes 11665408 | tf_op jit(solution)/shard_map/dot_general | solution.py:203
  175.2 7.0 %reduce-scatter.3.cloned.1.call-done = bf16[320,512]{1,0:T(8,128)(2,1)} async-done(((bf16[2560,512]{1,0:T(8,128)(2,1)}), bf16[320,512]{1,0:T(8,128)(2,1)}) %reduce-scatter.3.cloned.1.call-update) | async-done | bytes 327696 | tf_op jit(solution)/shard_map/reduce_scatter | solution.py:97
  182.2 4.9 %all-to-all-start.2 = ((bf16[4,80,512]{2,1,0:T(8,128)(2,1)}), bf16[4,80,512]{2,1,0:T(8,128)(2,1)}, u32[]{:S(2)}, u32[]{:S(2)}) async-start(bf16[4,80,512]{2,1,0:T(8,128)(2,1)} %bitcast.251), calls=%async_computation.3 | async-start | bytes 655360 | tf_op jit(solution)/shard_map/all_to_all | solution.py:104
  187.1 7.9 %convert_bitcast_fusion.2 = bf16[1,4096,1024]{2,1,0:T(8,128)(2,1)} fusion(bf16[320,4096]{1,0:T(8,128)(2,1)S(1)} %copy-done.2, bf16[320,1024]{1,0:T(8,128)(2,1)} %copy-done.37), kind=kOutput, calls=%fused_computation.14 | convolution fusion | flops 2688548864 | bytes 11665408 | tf_op jit(solution)/shard_map/dot_general | solution.py:200
  195.0 34.0 %reduce-scatter.5.cloned.1.call-done = bf16[320,512]{1,0:T(8,128)(2,1)} async-done(((bf16[2560,512]{1,0:T(8,128)(2,1)}), bf16[320,512]{1,0:T(8,128)(2,1)}) %reduce-scatter.5.cloned.1.call-update) | async-done | bytes 327696 | tf_op jit(solution)/shard_map/reduce_scatter | solution.py:97
  229.0 4.6 %all-to-all-start.3 = ((bf16[4,80,512]{2,1,0:T(8,128)(2,1)}), bf16[4,80,512]{2,1,0:T(8,128)(2,1)S(1)}, u32[]{:S(2)}, u32[]{:S(2)}) async-start(bf16[4,80,512]{2,1,0:T(8,128)(2,1)} %bitcast.248), calls=%async_computation.5 | async-start | bytes 655360 | tf_op jit(solution)/shard_map/all_to_all | solution.py:104
  233.6 1.4 fusion.73
  235.0 12.3 %all-gather.7 = f32[8,1,128]{2,1,0:T(1,128)S(1)} all-gather(f32[1,1,128]{2,1,0:T(1,128)S(1)} %bitcast.262), channel_id=5, replica_groups=mesh['ctx'=4,'exp'=4,'dp'=2] {'exp','dp'}, dimensions={0}, use_global_device_ids=true | all-gather | bytes 4608 | tf_op jit(solution)/shard_map/all_gather | solution.py:27
  247.4 1.1 fusion.155
  250.5 10.2 %all-gather.4 = bf16[32,66,64]{1,2,0:T(8,128)(2,1)S(1)} all-gather(bf16[8,66,64]{1,2,0:T(8,128)(2,1)S(1)} %pad_maximum_fusion.1), channel_id=6, replica_groups=mesh['ctx'=4,'exp'=4,'dp'=2] {'ctx'}, dimensions={0}, use_global_device_ids=true | all-gather | bytes 337920 | tf_op jit(solution)/shard_map/all_gather | solution.py:220
  265.7 14.2 %all-gather.8 = bf16[8,132,128]{2,1,0:T(8,128)(2,1)S(1)} all-gather(bf16[1,132,128]{2,1,0:T(8,128)(2,1)S(1)} %copy.179), channel_id=7, replica_groups=mesh['ctx'=4,'exp'=4,'dp'=2] {'exp','dp'}, dimensions={0}, use_global_device_ids=true | all-gather | bytes 304128 | tf_op jit(solution)/shard_map/all_gather | solution.py:27
  (175 shorter events, 25.5 us)
Async XLA Ops:
  7.2 23.1 %copy-start = (bf16[128,64]{0,1:T(8,128)(2,1)S(1)}, bf16[128,64]{0,1:T(8,128)(2,1)}, u32[]{:S(2)}) copy-start(bf16[128,64]{0,1:T(8,128)(2,1)} %param.14) | copy-start | bytes 49156
  7.2 36.7 %copy-start.8 = (bf16[128,64]{0,1:T(8,128)(2,1)S(1)}, bf16[128,64]{0,1:T(8,128)(2,1)}, u32[]{:S(2)}) copy-start(bf16[128,64]{0,1:T(8,128)(2,1)} %param.15) | copy-start | bytes 49156
  7.2 63.9 %all-gather.12.cloned.1.call-start = ((), (), s32[]{:S(2)}) async-start(), calls=%async_computation.8 | async-start | bytes 2949120 | tf_op jit(solution)/shard_map/all_gather | solution.py:93
  10.1 46.5 %copy-start.22 = (s32[128]{0:T(128)}, s32[128]{0:T(128)S(1)}, u32[]{:S(2)}) copy-start(s32[128]{0:T(128)S(1)} %get-tuple-element.112) | copy-start | bytes 1540
  10.1 46.5 %copy-start.24 = (s32[128]{0:T(128)}, s32[128]{0:T(128)S(1)}, u32[]{:S(2)}) copy-start(s32[128]{0:T(128)S(1)} %get-tuple-element.113) | copy-start | bytes 1540
  28.0 17.6 %copy-start.10 = (bf16[128,512]{1,0:T(8,128)(2,1)S(1)}, bf16[128,512]{1,0:T(8,128)(2,1)}, u32[]{:S(2)}) copy-start(bf16[128,512]{1,0:T(8,128)(2,1)} %param.12) | copy-start | bytes 393220
  28.0 72.0 %all-gather.14.cloned.1.call-start = ((), (), s32[]{:S(2)}) async-start(), calls=%async_computation.9 | async-start | bytes 2949120 | tf_op jit(solution)/shard_map/all_gather | solution.py:93
  29.1 27.5 %copy-start.21 = (f32[512]{0:T(512)S(1)}, f32[512]{0:T(512)}, u32[]{:S(2)}) copy-start(f32[512]{0:T(512)} %param.19) | copy-start | bytes 6148
  29.9 15.5 %copy-start.15 = (f32[128,8]{0,1:T(8,128)}, f32[128,8]{0,1:T(8,128)S(1)}, u32[]{:S(2)}) copy-start(f32[128,8]{0,1:T(8,128)S(1)} %fusion.130) | copy-start | bytes 12292
  30.2 126.3 %copy-start.11 = (f32[128,8]{0,1:T(8,128)}, f32[128,8]{0,1:T(8,128)S(1)}, u32[]{:S(2)}) copy-start(f32[128,8]{0,1:T(8,128)S(1)} %get-tuple-element.106) | copy-start | bytes 12292
  30.2 127.0 %copy-start.17 = (f32[128,8]{0,1:T(8,128)}, f32[128,8]{0,1:T(8,128)S(1)}, u32[]{:S(2)}) copy-start(f32[128,8]{0,1:T(8,128)S(1)} %get-tuple-element.107) | copy-start | bytes 12292
  56.6 14.6 %copy-start.26 = (f32[128]{0:T(128)}, f32[128]{0:T(128)S(1)}, u32[]{:S(2)}) copy-start(f32[128]{0:T(128)S(1)} %get-tuple-element.115) | copy-start | bytes 1540
  71.1 111.1 %reduce-scatter.3.cloned.1.call-start = ((), (), s32[]{:S(2)}) async-start(), calls=%async_computation.6 | async-start | bytes 2949120 | tf_op jit(solution)/shard_map/reduce_scatter | solution.py:97
  108.0 11.8 %slice-start.2 = ((s8[8388608]{0:T(1024)(128)(4,1)}), s8[4194304]{0:T(1024)(128)(4,1)S(1)}, s32[]{:S(2)}) async-start(s8[8388608]{0:T(1024)(128)(4,1)} %bitcast.267), calls=%async_computation.12 | async-start | bytes 8388608
  108.0 16.2 %slice-start = ((s8[8388608]{0:T(1024)(128)(4,1)}), s8[4194304]{0:T(1024)(128)(4,1)S(1)}, s32[]{:S(2)}) async-start(s8[8388608]{0:T(1024)(128)(4,1)} %bitcast.265), calls=%async_computation.10 | async-start | bytes 8388608
  114.3 10.0 %slice-start.1 = ((s8[8388608]{0:T(1024)(128)(4,1)}), s8[4194304]{0:T(1024)(128)(4,1)S(1)}, s32[]{:S(2)}) async-start(s8[8388608]{0:T(1024)(128)(4,1)} %bitcast.265), calls=%async_computation.11 | async-start | bytes 8388608
  138.4 90.6 %reduce-scatter.5.cloned.1.call-start = ((), (), s32[]{:S(2)}) async-start(), calls=%async_computation.7 | async-start | bytes 2949120 | tf_op jit(solution)/shard_map/reduce_scatter | solution.py:97
  158.1 10.3 %copy-start.2 = (bf16[320,4096]{1,0:T(8,128)(2,1)S(1)}, bf16[320,4096]{1,0:T(8,128)(2,1)}, u32[]{:S(2)}) copy-start(bf16[320,4096]{1,0:T(8,128)(2,1)} %reshape.243) | copy-start | bytes 7864324
  158.1 10.3 %copy-start.35 = (bf16[320,1024]{1,0:T(8,128)(2,1)S(1)}, bf16[320,1024]{1,0:T(8,128)(2,1)}, u32[]{:S(2)}) copy-start(bf16[320,1024]{1,0:T(8,128)(2,1)} %copy-done.34) | copy-start | bytes 1966084
  182.2 46.8 %all-to-all-start.2 = ((bf16[4,80,512]{2,1,0:T(8,128)(2,1)}), bf16[4,80,512]{2,1,0:T(8,128)(2,1)}, u32[]{:S(2)}, u32[]{:S(2)}) async-start(bf16[4,80,512]{2,1,0:T(8,128)(2,1)} %bitcast.251), calls=%async_computation.3 | async-start | bytes 655360 | tf_op jit(solution)/shard_map/all_to_all | solution.py:104
  187.1 60.3 %copy-start.4 = (bf16[128,512]{1,0:T(8,128)(2,1)S(1)}, bf16[128,512]{1,0:T(8,128)(2,1)}, u32[]{:S(2)}) copy-start(bf16[128,512]{1,0:T(8,128)(2,1)} %param.23) | copy-start | bytes 393220
  195.0 54.6 %copy-start.9 = (bf16[128,64]{0,1:T(8,128)(2,1)S(1)}, bf16[128,64]{0,1:T(8,128)(2,1)}, u32[]{:S(2)}) copy-start(bf16[128,64]{0,1:T(8,128)(2,1)} %param.15) | copy-start | bytes 49156
  195.0 54.6 %copy-start.18 = (f32[128,8]{0,1:T(8,128)S(1)}, f32[128,8]{0,1:T(8,128)}, u32[]{:S(2)}) copy-start(f32[128,8]{0,1:T(8,128)} %copy-done.17) | copy-start | bytes 12292
  229.0 32.9 %all-to-all-start.3 = ((bf16[4,80,512]{2,1,0:T(8,128)(2,1)}), bf16[4,80,512]{2,1,0:T(8,128)(2,1)S(1)}, u32[]{:S(2)}, u32[]{:S(2)}) async-start(bf16[4,80,512]{2,1,0:T(8,128)(2,1)} %bitcast.248), calls=%async_computation.5 | async-start | bytes 655360 | tf_op jit(solution)/shard_map/all_to_all | solution.py:104
  235.0 25.9 %copy-start.7 = (f32[128,8,64]{0,2,1:T(8,128)S(1)}, f32[128,8,64]{0,2,1:T(8,128)}, u32[]{:S(2)}) copy-start(f32[128,8,64]{0,2,1:T(8,128)} %copy-done.6) | copy-start | bytes 786436
  247.4 13.6 %copy-start.27 = (f32[8]{0:T(128)S(1)}, f32[8]{0:T(128)}, u32[]{:S(2)}) copy-start(f32[8]{0:T(128)} %get-tuple-element.89) | copy-start | bytes 100
  247.4 13.6 %copy-start.29 = (f32[8]{0:T(128)S(1)}, f32[8]{0:T(128)}, u32[]{:S(2)}) copy-start(f32[8]{0:T(128)} %copy-done.28) | copy-start | bytes 100
  247.4 13.6 %copy-start.31 = (f32[8]{0:T(128)S(1)}, f32[8]{0:T(128)}, u32[]{:S(2)}) copy-start(f32[8]{0:T(128)} %copy-done.30) | copy-start | bytes 100
  247.4 13.6 %copy-start.33 = (f32[8]{0:T(128)S(1)}, f32[8]{0:T(128)}, u32[]{:S(2)}) copy-start(f32[8]{0:T(128)} %copy-done.32) | copy-start | bytes 100
  249.4 12.6 %copy-start.25 = (s32[128]{0:T(128)S(1)}, s32[128]{0:T(128)}, u32[]{:S(2)}) copy-start(s32[128]{0:T(128)} %copy-done.24) | copy-start | bytes 1540
  250.1 12.2 %copy-start.23 = (s32[128]{0:T(128)S(1)}, s32[128]{0:T(128)}, u32[]{:S(2)}) copy-start(s32[128]{0:T(128)} %copy-done.22) | copy-start | bytes 1540
  263.4 17.8 %copy-start.12 = (f32[128,8]{0,1:T(8,128)S(1)}, f32[128,8]{0,1:T(8,128)}, u32[]{:S(2)}) copy-start(f32[128,8]{0,1:T(8,128)} %copy-done.11) | copy-start | bytes 12292
  (16 other events, 43.7 us)
Sparse Core Ops, SparseCore 0:
  28.1 30.6 all-gather.11
  71.2 28.7 all-gather.13
  138.5 43.6 reduce-scatter.2
  185.4 43.6 reduce-scatter.4

commit v3 on v2

--- a/solution.py
+++ b/solution.py
@@ -76,15 +76,20 @@
 def arrange_rows(gathered, ctx_count, dp_count):
     exp_count, capacity, feat = gathered.shape[1:]
     shaped = gathered.reshape(ctx_count, dp_count, exp_count, capacity, feat)
-    return shaped.transpose(0, 3, 2, 1, 4).reshape(
-        ctx_count * capacity, exp_count * dp_count * feat
-    )
+    blocks = [
+        shaped[:, d, e].reshape(ctx_count * capacity, feat)
+        for e in range(exp_count)
+        for d in range(dp_count)
+    ]
+    return jnp.concatenate(blocks, axis=1)
 
 
 def arrange_sums(full_term, ctx_count, dp_count, exp_count, capacity):
     feat = full_term.shape[1] // (exp_count * dp_count)
-    shaped = full_term.reshape(ctx_count, capacity, exp_count, dp_count, feat)
-    return shaped.transpose(0, 3, 2, 1, 4).reshape(-1, feat)
+    shaped = full_term.reshape(ctx_count, capacity, -1)
+    starts = [(e * dp_count + d) * feat for d in range(dp_count) for e in range(exp_count)]
+    blocks = [shaped[:, None, :, start : start + feat] for start in starts]
+    return jnp.concatenate(blocks, axis=1).reshape(-1, feat)
 
 
 def expert_rows(rows, expert_count, ctx_count, dp_count):
@@ -93,16 +98,19 @@
     return arrange_rows(lax.all_gather(got, ("ctx", "dp")), ctx_count, dp_count)
 
 
-def token_rows(full_term, ctx_count, dp_count, exp_count, capacity):
-    total = lax.psum_scatter(
+def summed_rows(full_term, ctx_count, dp_count, exp_count, capacity):
+    return lax.psum_scatter(
         arrange_sums(full_term, ctx_count, dp_count, exp_count, capacity),
         ("ctx", "dp"),
         scatter_dimension=0,
         tiled=True,
     )
+
+
+def token_rows(total, exp_count):
     feat = total.shape[1]
     back = lax.all_to_all(
-        total.reshape(exp_count, capacity, feat), "exp", split_axis=0, concat_axis=0, tiled=True
+        total.reshape(exp_count, -1, feat), "exp", split_axis=0, concat_axis=0, tiled=True
     )
     return back.reshape(-1, feat)
 
@@ -184,19 +192,16 @@
         grad_up, w_up[0], (((1,), (1,)), ((), ())), preferred_element_type=jnp.float32
     )
     full_back, later_act = lax.optimization_barrier((full_back.astype(jnp.bfloat16), hidden_act))
-    back_in = token_rows(full_back, ctx_count, dp_count, exp_count, capacity)
+    back_total = summed_rows(full_back, ctx_count, dp_count, exp_count, capacity)
+    back_in = token_rows(back_total, exp_count)
     full_out = lax.dot_general(
         later_act, w_down[0], (((1,), (1,)), ((), ())), preferred_element_type=jnp.float32
     )
-    back_out = token_rows(full_out.astype(jnp.bfloat16), ctx_count, dp_count, exp_count, capacity)
+    out_total = summed_rows(
+        full_out.astype(jnp.bfloat16), ctx_count, dp_count, exp_count, capacity
+    )
     grad_normed = rows_back(select, back_in)
     out_f = out_grad.astype(jnp.float32)
-    probs_part = jnp.stack(
-        [
-            jnp.sum(rows_back(first.astype(jnp.bfloat16), back_out) * out_f, axis=1),
-            jnp.sum(rows_back(second.astype(jnp.bfloat16), back_out) * out_f, axis=1),
-        ]
-    )
     w_gate_grad = jnp.dot(rows_flat.T, grad_gate, preferred_element_type=jnp.float32).astype(
         jnp.bfloat16
     )[None]
@@ -225,6 +230,14 @@
         jnp.sum(carries[:, :, head_size:].astype(jnp.float32), axis=0), 2, axis=1
     )
     grad_gain = (gain_high + gain_low).reshape(feat)
+    grad_state, out_total = lax.optimization_barrier((grad_state, out_total))
+    back_out = token_rows(out_total, exp_count)
+    probs_part = jnp.stack(
+        [
+            jnp.sum(rows_back(first.astype(jnp.bfloat16), back_out) * out_f, axis=1),
+            jnp.sum(rows_back(second.astype(jnp.bfloat16), back_out) * out_f, axis=1),
+        ]
+    )
     grad_total = jnp.sum(grad_state * state_in, axis=(1, 2))
     vals_second, keys_second, decay_second = state_pull((grad_total, grad_state))
     both = jnp.concatenate([keys_first + keys_second, queries_part], axis=1).astype(jnp.bfloat16)

time: 299 us -> 265 us (0.89); the launches traced: 293 us -> 265 us
  local copies, waits for them, and re-layouts: 40.6 us -> 19.7 us
  matrix products: 69.9 us -> 63.6 us
    reshape x6 -> x0, local copies, waits for them, and re-layouts: 21 us -> none  [the longest x4 13.7 us: arrange_sums(): shaped = full_term.reshape(ctx_count, capacity, exp_count, dp_count, feat)]
    reduce_scatter x2, waiting for transfers between devices: 41 us -> 27.6 us  [summed_rows(): lax.psum_scatter(arrange_sums(full_term, ctx_count, dp_count, exp_count,...]
    transpose x2 -> x0, local copies, waits for them, and re-layouts: 8.87 us -> none  [arrange_rows(): shaped.transpose(0, 3, 2, 1, 4)]
    all_to_all x2, waiting for transfers between devices: 0.01 us -> 7.15 us  [token_rows(): lax.all_to_all(total.reshape(exp_count, -1, feat), 'exp', split_axis=0, c...]
    all_gather x2, waiting for transfers between devices: 20.7 us -> 26.7 us  [expert_rows(): return arrange_rows(lax.all_gather(got, ('ctx', 'dp')), ctx_count, dp_count)]
    unnamed x93 -> x131, local copies, waits for them, and re-layouts: 6.4 us -> 11.6 us
    slice x0 -> x2, local copies, waits for them, and re-layouts: none -> 3.79 us  [arrange_rows(): shaped[:, d, e].reshape(ctx_count * capacity, feat)]
    dot_general x1, matrix products: 10.3 us -> 6.52 us  [per_device(): lax.dot_general(later_act, w_down[0], (((1,), (1,)), ((), ())), preferred...]
  transfers between devices with their start and end apart: 6 -> 6, of which waited for: 3 -> 5; matrix products, arithmetic and copies ran while one was open for 22% -> 18% of each run, Pallas kernels for 0% -> 0%
where the time goes in v3:
time: 265 us
  blocking collectives  90.2 us (34%)
  matrix products  63.6 us (24%)
  waiting for transfers between devices  61.6 us (23%)
  local copies, waits for them, and re-layouts  19.7 us (7%)
  between operations  14.8 us (6%)
  starting transfers between devices  9.76 us (4%)
  other arithmetic  5.01 us (2%)
    all_gather x3, blocking collectives, sum_over(): return jnp.sum(lax.all_gather(x, axes).astype(jnp.float32), axis=0)  35.4 us
    all_to_all x2, blocking collectives, expert_rows(): got = lax.all_to_all(send, 'exp', split_axis=0, concat_axis=0, tiled=True)  30.6 us
    reduce_scatter x2, waiting for transfers between devices, summed_rows(): lax.psum_scatter(arrange_sums(full_term, ctx_count, dp_count, exp_count,...  27.6 us
    all_gather x2, waiting for transfers between devices, expert_rows(): return arrange_rows(lax.all_gather(got, ('ctx', 'dp')), ctx_count, dp_count)  26.7 us
    all_gather x1, blocking collectives, per_device(): lax.all_gather(jnp.concatenate([state_local, decay_row], axis=1).astype(j...  12.1 us
    all_gather x1, blocking collectives, per_device(): lax.all_gather(jnp.concatenate([carry_cot.astype(jnp.bfloat16)] + gain_ro...  12.1 us
    unnamed x131, local copies, waits for them, and re-layouts  11.6 us
    dot_general x1, matrix products, per_device(): jnp.dot(cot_flat.T, hidden_act, preferred_element_type=jnp.float32)  10.2 us
  transfers between devices with their start and end apart: 6, of which 5 were waited for; matrix products, arithmetic and copies ran while one was open for 18% of the time, Pallas kernels for 0%

profile of v3, /device:TPU:0, one launch (start us, length us, event | category | flops | bytes accessed | tf_op | source)
XLA Modules:
  0.0 264.6 jit_solution(16623416274434121643)
XLA Ops:
  10.3 1.1 fusion.22
  11.4 16.5 %all_to_all.20 = bf16[4,80,512]{2,1,0:T(8,128)(2,1)} all-to-all(bf16[4,80,512]{2,1,0:T(8,128)(2,1)S(1)} %bitcast.344), channel_id=1, replica_groups=mesh['ctx'=4,'exp'=4,'dp'=2] {'exp'}, dimensions={0} | all-to-all | bytes 655360 | tf_op jit(solution)/shard_map/all_to_all | solution.py:97
  28.0 1.0 copy.204
  31.0 12.1 %all_gather.40 = bf16[4,8,65,64]{2,3,1,0:T(8,128)(2,1)S(1)} all-gather(bf16[1,8,65,64]{2,3,1,0:T(8,128)(2,1)S(1)} %pad_maximum_fusion), channel_id=1, replica_groups=mesh['ctx'=4,'exp'=4,'dp'=2] {'ctx'}, dimensions={0}, use_global_device_ids=true | all-gather | bytes 332800 | tf_op jit(solution)/shard_map/all_gather | solution.py:153
  45.8 10.3 %all-gather.6 = f32[8,1,128]{2,1,0:T(1,128)S(1)} all-gather(f32[1,1,128]{2,1,0:T(1,128)S(1)} %bitcast.357), channel_id=2, replica_groups=mesh['ctx'=4,'exp'=4,'dp'=2] {'exp','dp'}, dimensions={0}, use_global_device_ids=true | all-gather | bytes 4608 | tf_op jit(solution)/shard_map/all_gather | solution.py:27
  57.0 14.1 %all_to_all.21 = bf16[4,80,512]{2,1,0:T(8,128)(2,1)} all-to-all(bf16[4,80,512]{2,1,0:T(8,128)(2,1)S(1)} %bitcast.345), channel_id=1, replica_groups=mesh['ctx'=4,'exp'=4,'dp'=2] {'exp'}, dimensions={0} | all-to-all | bytes 655360 | tf_op jit(solution)/shard_map/all_to_all | solution.py:97
  71.3 2.0 fusion.151
  73.3 26.7 %all-gather.14.cloned.1.call-done = bf16[32,80,512]{2,1,0:T(8,128)(2,1)} async-done(((bf16[4,80,512]{2,1,0:T(8,128)(2,1)}), bf16[32,80,512]{2,1,0:T(8,128)(2,1)}) %all-gather.14.cloned.1.call-update) | async-done | bytes 2621456 | tf_op jit(solution)/shard_map/all_gather | solution.py:98
  100.0 1.8 fusion.152
  102.3 6.3 %fusion.2 = f32[320,1024]{1,0:T(8,128)S(1)} fusion(bf16[320,4096]{1,0:T(8,128)(2,1)S(1)} %constant_dynamic-update-slice_fusion.8, bf16[1,4096,1024]{2,1,0:T(8,128)(2,1)} %param.20), kind=kOutput, calls=%fused_computation.2 | convolution fusion | flops 2684354560 | bytes 12320768 | tf_op jit(solution)/shard_map/dot_general | solution.py:182
  108.9 1.5 copy-done.15
  110.4 3.0 %fusion.10 = f32[320,1024]{1,0:T(8,128)S(1)} fusion(bf16[320,4096]{1,0:T(8,128)(2,1)S(1)} %constant_dynamic-update-slice_fusion, bf16[1,4096,1024]{2,1,0:T(8,128)(2,1)S(1)} %bitcast.368), kind=kOutput, calls=%fused_computation.10 | convolution fusion | flops 2684354560 | bytes 12320768 | tf_op jit(solution)/shard_map/dot_general | solution.py:186
  113.4 1.1 slice-done.3
  114.5 4.5 %multiply_convert_fusion = (bf16[320,1024]{1,0:T(8,128)(2,1)}, bf16[320,1024]{1,0:T(8,128)(2,1)S(1)}, bf16[320,1024]{1,0:T(8,128)(2,1)}) fusion(f32[320,1024]{1,0:T(8,128)S(1)} %fusion.2, f32[320,1024]{1,0:T(8,128)S(1)} %fusion.10, bf16[320,4096]{1,0:T(8,128)(2,1)S(1)} %constant_dynamic-update-slice_fusion.8, bf16[1,4096,1024]{2,1,0:T(8,128)(2,1)S(1)} %bitcast.366), kind=kOutput, calls=%fused_computation.18 | convolution fusion | flops 2689269760 | bytes 15597568 | tf_op jit(solution)/shard_map/dot_general | solution.py:183
  119.0 2.9 %fusion = f32[320,4096]{1,0:T(8,128)S(1)} fusion(bf16[320,1024]{1,0:T(8,128)(2,1)S(1)} %get-tuple-element.102, bf16[1,4096,1024]{2,1,0:T(8,128)(2,1)S(1)} %bitcast.364), kind=kOutput, calls=%fused_computation | convolution fusion | flops 2684354560 | bytes 14286848 | tf_op jit(solution)/shard_map/dot_general | solution.py:189
  121.9 4.3 %fusion.15 = bf16[320,4096]{1,0:T(8,128)(2,1)S(1)} fusion(f32[320,4096]{1,0:T(8,128)S(1)} %fusion, bf16[320,1024]{1,0:T(8,128)(2,1)} %get-tuple-element.103, bf16[1,4096,1024]{2,1,0:T(8,128)(2,1)S(1)} %bitcast.366), kind=kOutput, calls=%fused_computation.16 | convolution fusion | flops 2686976000 | bytes 16908288 | tf_op jit(solution)/shard_map/dot_general | solution.py:191
  126.5 1.5 copy-done.1
  128.2 6.5 %fusion.18 = bf16[320,4096]{1,0:T(8,128)(2,1)S(1)} fusion(bf16[320,1024]{1,0:T(8,128)(2,1)} %get-tuple-element.15, bf16[1,4096,1024]{2,1,0:T(8,128)(2,1)} %param.22), kind=kOutput, calls=%fused_computation.17 | convolution fusion | flops 2685665280 | bytes 11665408 | tf_op jit(solution)/shard_map/dot_general | solution.py:197
  135.0 1.5 copy-done.2
  137.4 10.2 %convert_bitcast_fusion = bf16[1,4096,1024]{2,1,0:T(8,128)(2,1)} fusion(bf16[320,4096]{1,0:T(8,128)(2,1)} %copy-done.15, bf16[320,1024]{1,0:T(8,128)(2,1)} %get-tuple-element.15), kind=kOutput, calls=%fused_computation.12 | convolution fusion | flops 2688548864 | bytes 11665408 | tf_op jit(solution)/shard_map/dot_general | solution.py:211
  147.7 6.8 %convert_bitcast_fusion.1 = bf16[1,4096,1024]{2,1,0:T(8,128)(2,1)} fusion(bf16[320,4096]{1,0:T(8,128)(2,1)S(1)} %copy-done.17, bf16[320,1024]{1,0:T(8,128)(2,1)S(1)} %copy-done.38), kind=kOutput, calls=%fused_computation.13 | convolution fusion | flops 2688548864 | bytes 11665408 | tf_op jit(solution)/shard_map/dot_general | solution.py:208
  154.5 17.3 %reduce-scatter.3.cloned.1.call-done = bf16[320,512]{1,0:T(8,128)(2,1)} async-done(((bf16[2560,512]{1,0:T(8,128)(2,1)}), bf16[320,512]{1,0:T(8,128)(2,1)}) %reduce-scatter.3.cloned.1.call-update) | async-done | bytes 327696 | tf_op jit(solution)/shard_map/reduce_scatter | solution.py:102
  171.8 4.6 %all-to-all-start.2 = ((bf16[4,80,512]{2,1,0:T(8,128)(2,1)}), bf16[4,80,512]{2,1,0:T(8,128)(2,1)S(1)}, u32[]{:S(2)}, u32[]{:S(2)}) async-start(bf16[4,80,512]{2,1,0:T(8,128)(2,1)} %bitcast.347), calls=%async_computation.3 | async-start | bytes 655360 | tf_op jit(solution)/shard_map/all_to_all | solution.py:112
  176.5 8.7 %convert_bitcast_fusion.2 = bf16[1,4096,1024]{2,1,0:T(8,128)(2,1)} fusion(bf16[320,4096]{1,0:T(8,128)(2,1)} %copy-done.16, bf16[320,1024]{1,0:T(8,128)(2,1)S(1)} %copy-done.40), kind=kOutput, calls=%fused_computation.14 | convolution fusion | flops 2688548864 | bytes 11665408 | tf_op jit(solution)/shard_map/dot_general | solution.py:205
  185.1 1.6 all-to-all-done.2
  187.2 10.8 %all-gather.7 = f32[8,1,128]{2,1,0:T(1,128)S(1)} all-gather(f32[1,1,128]{2,1,0:T(1,128)S(1)} %bitcast.360), channel_id=5, replica_groups=mesh['ctx'=4,'exp'=4,'dp'=2] {'exp','dp'}, dimensions={0}, use_global_device_ids=true | all-gather | bytes 4608 | tf_op jit(solution)/shard_map/all_gather | solution.py:27
  199.5 12.1 %all-gather.4 = bf16[32,66,64]{1,2,0:T(8,128)(2,1)S(1)} all-gather(bf16[8,66,64]{1,2,0:T(8,128)(2,1)S(1)} %pad_maximum_fusion.1), channel_id=6, replica_groups=mesh['ctx'=4,'exp'=4,'dp'=2] {'ctx'}, dimensions={0}, use_global_device_ids=true | all-gather | bytes 337920 | tf_op jit(solution)/shard_map/all_gather | solution.py:225
  212.1 10.3 %reduce-scatter.5.cloned.1.call-done = bf16[320,512]{1,0:T(8,128)(2,1)} async-done(((bf16[2560,512]{1,0:T(8,128)(2,1)}), bf16[320,512]{1,0:T(8,128)(2,1)}) %reduce-scatter.5.cloned.1.call-update) | async-done | bytes 327696 | tf_op jit(solution)/shard_map/reduce_scatter | solution.py:102
  224.2 0.9 fusion.55
  225.2 4.6 %all-to-all-start.3 = ((bf16[4,80,512]{2,1,0:T(8,128)(2,1)}), bf16[4,80,512]{2,1,0:T(8,128)(2,1)S(1)}, u32[]{:S(2)}, u32[]{:S(2)}) async-start(bf16[4,80,512]{2,1,0:T(8,128)(2,1)} %bitcast.91), calls=%async_computation.5 | async-start | bytes 655360 | tf_op jit(solution)/shard_map/all_to_all | solution.py:112
  234.5 5.6 %all-to-all-done.3 = bf16[4,80,512]{2,1,0:T(8,128)(2,1)S(1)} async-done(((bf16[4,80,512]{2,1,0:T(8,128)(2,1)}), bf16[4,80,512]{2,1,0:T(8,128)(2,1)S(1)}, u32[]{:S(2)}, u32[]{:S(2)}) %all-to-all-start.3) | async-done | bytes 327712 | tf_op jit(solution)/shard_map/all_to_all | solution.py:112
  241.3 14.2 %all-gather.8 = bf16[8,132,128]{2,1,0:T(8,128)(2,1)S(1)} all-gather(bf16[1,132,128]{2,1,0:T(8,128)(2,1)S(1)} %copy.231), channel_id=7, replica_groups=mesh['ctx'=4,'exp'=4,'dp'=2] {'exp','dp'}, dimensions={0}, use_global_device_ids=true | all-gather | bytes 304128 | tf_op jit(solution)/shard_map/all_gather | solution.py:27
  (211 shorter events, 23.4 us)
Async XLA Ops:
  7.2 23.0 %copy-start = (bf16[128,64]{0,1:T(8,128)(2,1)S(1)}, bf16[128,64]{0,1:T(8,128)(2,1)}, u32[]{:S(2)}) copy-start(bf16[128,64]{0,1:T(8,128)(2,1)} %param.14) | copy-start | bytes 49156
  7.2 36.7 %copy-start.6 = (bf16[128,64]{0,1:T(8,128)(2,1)S(1)}, bf16[128,64]{0,1:T(8,128)(2,1)}, u32[]{:S(2)}) copy-start(bf16[128,64]{0,1:T(8,128)(2,1)} %param.15) | copy-start | bytes 49156
  7.2 64.1 %all-gather.12.cloned.1.call-start = ((), (), s32[]{:S(2)}) async-start(), calls=%async_computation.8 | async-start | bytes 2949120 | tf_op jit(solution)/shard_map/all_gather | solution.py:98
  10.1 46.5 %copy-start.24 = (s32[128]{0:T(128)}, s32[128]{0:T(128)S(1)}, u32[]{:S(2)}) copy-start(s32[128]{0:T(128)S(1)} %get-tuple-element.132) | copy-start | bytes 1540
  10.1 46.5 %copy-start.26 = (s32[128]{0:T(128)}, s32[128]{0:T(128)S(1)}, u32[]{:S(2)}) copy-start(s32[128]{0:T(128)S(1)} %get-tuple-element.133) | copy-start | bytes 1540
  27.9 17.7 %copy-start.8 = (bf16[128,512]{1,0:T(8,128)(2,1)S(1)}, bf16[128,512]{1,0:T(8,128)(2,1)}, u32[]{:S(2)}) copy-start(bf16[128,512]{1,0:T(8,128)(2,1)} %param.12) | copy-start | bytes 393220
  28.0 28.7 %copy-start.22 = (f32[512]{0:T(512)S(1)}, f32[512]{0:T(512)}, u32[]{:S(2)}) copy-start(f32[512]{0:T(512)} %param.19) | copy-start | bytes 6148
  28.0 72.0 %all-gather.14.cloned.1.call-start = ((), (), s32[]{:S(2)}) async-start(), calls=%async_computation.9 | async-start | bytes 2949120 | tf_op jit(solution)/shard_map/all_gather | solution.py:98
  29.9 15.6 %copy-start.13 = (f32[128,8]{0,1:T(8,128)}, f32[128,8]{0,1:T(8,128)S(1)}, u32[]{:S(2)}) copy-start(f32[128,8]{0,1:T(8,128)S(1)} %fusion.126) | copy-start | bytes 12292
  30.2 15.2 %copy-start.18 = (f32[128,8]{0,1:T(8,128)}, f32[128,8]{0,1:T(8,128)S(1)}, u32[]{:S(2)}) copy-start(f32[128,8]{0,1:T(8,128)S(1)} %get-tuple-element.127) | copy-start | bytes 12292
  45.8 25.6 %copy-start.3 = (bf16[128,512]{1,0:T(8,128)(2,1)}, bf16[128,512]{1,0:T(8,128)(2,1)S(1)}, u32[]{:S(2)}) copy-start(bf16[128,512]{1,0:T(8,128)(2,1)S(1)} %get-tuple-element.100) | copy-start | bytes 393220
  56.6 14.7 %copy-start.33 = (f32[128]{0:T(128)}, f32[128]{0:T(128)S(1)}, u32[]{:S(2)}) copy-start(f32[128]{0:T(128)S(1)} %get-tuple-element.135) | copy-start | bytes 1540
  71.1 100.7 %reduce-scatter.3.cloned.1.call-start = ((), (), s32[]{:S(2)}) async-start(), calls=%async_computation.6 | async-start | bytes 2949120 | tf_op jit(solution)/shard_map/reduce_scatter | solution.py:102
  102.2 11.1 %copy-start.16 = (bf16[320,4096]{1,0:T(8,128)(2,1)}, bf16[320,4096]{1,0:T(8,128)(2,1)S(1)}, u32[]{:S(2)}) copy-start(bf16[320,4096]{1,0:T(8,128)(2,1)S(1)} %constant_dynamic-update-slice_fusion.8) | copy-start | bytes 7864324
  128.0 94.5 %reduce-scatter.5.cloned.1.call-start = ((), (), s32[]{:S(2)}) async-start(), calls=%async_computation.7 | async-start | bytes 2949120 | tf_op jit(solution)/shard_map/reduce_scatter | solution.py:102
  147.7 28.7 %copy-start.40 = (bf16[320,1024]{1,0:T(8,128)(2,1)S(1)}, bf16[320,1024]{1,0:T(8,128)(2,1)}, u32[]{:S(2)}) copy-start(bf16[320,1024]{1,0:T(8,128)(2,1)} %copy-done.39) | copy-start | bytes 1966084
  171.8 14.9 %all-to-all-start.2 = ((bf16[4,80,512]{2,1,0:T(8,128)(2,1)}), bf16[4,80,512]{2,1,0:T(8,128)(2,1)S(1)}, u32[]{:S(2)}, u32[]{:S(2)}) async-start(bf16[4,80,512]{2,1,0:T(8,128)(2,1)} %bitcast.347), calls=%async_computation.3 | async-start | bytes 655360 | tf_op jit(solution)/shard_map/all_to_all | solution.py:112
  176.4 10.3 %copy-start.4 = (bf16[128,512]{1,0:T(8,128)(2,1)S(1)}, bf16[128,512]{1,0:T(8,128)(2,1)}, u32[]{:S(2)}) copy-start(bf16[128,512]{1,0:T(8,128)(2,1)} %copy-done.3) | copy-start | bytes 393220
  176.4 10.3 %copy-start.23 = (f32[512]{0:T(512)S(1)}, f32[512]{0:T(512)}, u32[]{:S(2)}) copy-start(f32[512]{0:T(512)} %param.19) | copy-start | bytes 6148
  176.4 21.9 %copy-start.5 = (bf16[128,512]{1,0:T(8,128)(2,1)S(1)}, bf16[128,512]{1,0:T(8,128)(2,1)}, u32[]{:S(2)}) copy-start(bf16[128,512]{1,0:T(8,128)(2,1)} %param.23) | copy-start | bytes 393220
  176.5 21.9 %copy-start.37 = (f32[128]{0:T(128)S(1)}, f32[128]{0:T(128)}, u32[]{:S(2)}) copy-start(f32[128]{0:T(128)} %get-tuple-element.134) | copy-start | bytes 1540
  185.1 13.7 %copy-start.7 = (bf16[128,64]{0,1:T(8,128)(2,1)S(1)}, bf16[128,64]{0,1:T(8,128)(2,1)}, u32[]{:S(2)}) copy-start(bf16[128,64]{0,1:T(8,128)(2,1)} %param.15) | copy-start | bytes 49156
  185.1 13.7 %copy-start.19 = (f32[128,8]{0,1:T(8,128)S(1)}, f32[128,8]{0,1:T(8,128)}, u32[]{:S(2)}) copy-start(f32[128,8]{0,1:T(8,128)} %copy-done.18) | copy-start | bytes 12292
  187.1 24.7 %copy-start.29 = (f32[8]{0:T(128)S(1)}, f32[8]{0:T(128)}, u32[]{:S(2)}) copy-start(f32[8]{0:T(128)} %copy-done.28) | copy-start | bytes 100
  187.2 24.7 %copy-start.31 = (f32[8]{0:T(128)S(1)}, f32[8]{0:T(128)}, u32[]{:S(2)}) copy-start(f32[8]{0:T(128)} %copy-done.30) | copy-start | bytes 100
  187.2 24.7 %copy-start.32 = (f32[8]{0:T(128)S(1)}, f32[8]{0:T(128)}, u32[]{:S(2)}) copy-start(f32[8]{0:T(128)} %get-tuple-element.93) | copy-start | bytes 100
  198.3 24.1 %copy-start.36 = (f32[8]{0:T(128)S(1)}, f32[8]{0:T(128)}, u32[]{:S(2)}) copy-start(f32[8]{0:T(128)} %copy-done.35) | copy-start | bytes 100
  198.5 24.2 %copy-start.10 = (f32[128,8]{0,1:T(8,128)S(1)}, f32[128,8]{0,1:T(8,128)}, u32[]{:S(2)}) copy-start(f32[128,8]{0,1:T(8,128)} %copy-done.9) | copy-start | bytes 12292
  211.6 12.6 %copy-start.12 = (f32[128,128]{1,0:T(8,128)S(1)}, f32[128,128]{1,0:T(8,128)}, u32[]{:S(2)}) copy-start(f32[128,128]{1,0:T(8,128)} %copy-done.11) | copy-start | bytes 196612
  211.6 12.6 %copy-start.14 = (f32[128,8]{0,1:T(8,128)S(1)}, f32[128,8]{0,1:T(8,128)}, u32[]{:S(2)}) copy-start(f32[128,8]{0,1:T(8,128)} %copy-done.13) | copy-start | bytes 12292
  211.6 12.6 %copy-start.21 = (pred[128,128]{1,0:T(8,128)(4,1)S(1)}, pred[128,128]{1,0:T(8,128)(4,1)}, u32[]{:S(2)}) copy-start(pred[128,128]{1,0:T(8,128)(4,1)} %copy-done.20) | copy-start | bytes 49156
  225.2 14.9 %all-to-all-start.3 = ((bf16[4,80,512]{2,1,0:T(8,128)(2,1)}), bf16[4,80,512]{2,1,0:T(8,128)(2,1)S(1)}, u32[]{:S(2)}, u32[]{:S(2)}) async-start(bf16[4,80,512]{2,1,0:T(8,128)(2,1)} %bitcast.91), calls=%async_computation.5 | async-start | bytes 655360 | tf_op jit(solution)/shard_map/all_to_all | solution.py:112
  (21 other events, 109.0 us)
Sparse Core Ops, SparseCore 0:
  28.1 30.6 all-gather.11
  71.2 28.7 all-gather.13
  128.1 43.6 reduce-scatter.2
  175.0 47.4 reduce-scatter.4

commit v4 on v3

--- a/solution.py
+++ b/solution.py
@@ -95,7 +95,7 @@
 def expert_rows(rows, expert_count, ctx_count, dp_count):
     send = rows.reshape(expert_count, -1, rows.shape[1])
     got = lax.all_to_all(send, "exp", split_axis=0, concat_axis=0, tiled=True)
-    return arrange_rows(lax.all_gather(got, ("ctx", "dp")), ctx_count, dp_count)
+    return (got, arrange_rows(lax.all_gather(got, ("ctx", "dp")), ctx_count, dp_count))
 
 
 def summed_rows(full_term, ctx_count, dp_count, exp_count, capacity):
@@ -176,9 +176,9 @@
     )
     cot_rows = jnp.dot(select, out_grad, preferred_element_type=jnp.float32)
     cot_rows = (row_prob[:, None] * cot_rows).astype(jnp.bfloat16)
-    cot_flat = expert_rows(cot_rows, expert_count, ctx_count, dp_count)
+    got_cot, cot_flat = expert_rows(cot_rows, expert_count, ctx_count, dp_count)
     send_rows = jnp.dot(select, normed, preferred_element_type=jnp.float32).astype(jnp.bfloat16)
-    rows_flat = expert_rows(send_rows, expert_count, ctx_count, dp_count)
+    _, rows_flat = expert_rows(send_rows, expert_count, ctx_count, dp_count)
     act_gate = jnp.dot(rows_flat, w_gate[0], preferred_element_type=jnp.float32)
     act_up = jnp.dot(rows_flat, w_up[0], preferred_element_type=jnp.float32)
     swish_val, swish_slope = silu_parts(act_gate)
@@ -201,7 +201,6 @@
         full_out.astype(jnp.bfloat16), ctx_count, dp_count, exp_count, capacity
     )
     grad_normed = rows_back(select, back_in)
-    out_f = out_grad.astype(jnp.float32)
     w_gate_grad = jnp.dot(rows_flat.T, grad_gate, preferred_element_type=jnp.float32).astype(
         jnp.bfloat16
     )[None]
@@ -231,21 +230,24 @@
     )
     grad_gain = (gain_high + gain_low).reshape(feat)
     grad_state, out_total = lax.optimization_barrier((grad_state, out_total))
-    back_out = token_rows(out_total, exp_count)
-    probs_part = jnp.stack(
-        [
-            jnp.sum(rows_back(first.astype(jnp.bfloat16), back_out) * out_f, axis=1),
-            jnp.sum(rows_back(second.astype(jnp.bfloat16), back_out) * out_f, axis=1),
-        ]
+    probs_part = jnp.sum(
+        out_total.reshape(got_cot.shape).astype(jnp.float32) * got_cot.astype(jnp.float32),
+        axis=(0, 2),
     )
     grad_total = jnp.sum(grad_state * state_in, axis=(1, 2))
     vals_second, keys_second, decay_second = state_pull((grad_total, grad_state))
     both = jnp.concatenate([keys_first + keys_second, queries_part], axis=1).astype(jnp.bfloat16)
-    probs_rows = jnp.concatenate(two_parts(probs_part)).reshape(-1, both.shape[1])
-    summed = sum_over(jnp.concatenate([both, probs_rows]), ("exp", "dp"))
-    grad_keys, grad_queries = summed[:tokens, :width], summed[:tokens, width:]
-    probs_high, probs_low = jnp.split(summed[tokens:].reshape(4, tokens), 2)
-    grad_probs = (probs_high + probs_low).T
+    probs_flat = jnp.concatenate(two_parts(probs_part))
+    probs_flat = jnp.pad(probs_flat, (0, -probs_flat.shape[0] % both.shape[1]))
+    ends = lax.all_gather(
+        jnp.concatenate([both, probs_flat.reshape(-1, both.shape[1])]), ("exp", "dp")
+    ).astype(jnp.float32)
+    summed = jnp.sum(ends[:, :tokens], axis=0)
+    grad_keys, grad_queries = summed[:, :width], summed[:, width:]
+    parts = ends[:, tokens:].reshape(exp_count, dp_count, -1)[:, :, : 2 * capacity]
+    parts = parts.reshape(exp_count, dp_count, 2, capacity).sum(axis=(1, 2)).reshape(-1, 1)
+    pair_sums = [jnp.sum(jnp.where(m, parts, 0.0), axis=0) for m in (first, second)]
+    grad_probs = jnp.stack(pair_sums, axis=1) / gate_probs
     grad_residual = grad_hidden.astype(jnp.bfloat16)
     grad_values = (vals_first + vals_second).reshape(tokens, feat).astype(jnp.bfloat16)
     grad_decay = decay_first + decay_second

time: 265 us -> 253 us (0.955)
  waiting for transfers between devices: 61.6 us -> 54.9 us
  starting transfers between devices: 9.76 us -> 5.15 us
    all_gather x0 -> x1, blocking collectives: none -> 14.3 us  [per_device(): lax.all_gather(jnp.concatenate([both, probs_flat.reshape(-1, both.shape[1...]
    all_gather x3 -> x2, blocking collectives: 35.4 us -> 21.1 us  [sum_over(): return jnp.sum(lax.all_gather(x, axes).astype(jnp.float32), axis=0)]
    all_to_all x2 -> x1, waiting for transfers between devices: 7.15 us -> 1.59 us  [token_rows(): lax.all_to_all(total.reshape(exp_count, -1, feat), 'exp', split_axis=0, c...]
    all_to_all x2 -> x1, starting transfers between devices: 9.2 us -> 4.58 us  [token_rows(): lax.all_to_all(total.reshape(exp_count, -1, feat), 'exp', split_axis=0, c...]
    unnamed x131 -> x134, local copies, waits for them, and re-layouts: 11.6 us -> 10.8 us
  transfers between devices with their start and end apart: 6 -> 5, of which waited for: 5 -> 4; matrix products, arithmetic and copies ran while one was open for 18% -> 18% of each run, Pallas kernels for 0% -> 0%
where the time goes in v4:
time: 253 us; the launch traced here: 252 us
  blocking collectives  89.9 us (36%)
  matrix products  62.9 us (25%)
  waiting for transfers between devices  54.9 us (22%)
  local copies, waits for them, and re-layouts  19 us (8%)
  between operations  14.8 us (6%)
  other arithmetic  5.82 us (2%)
  starting transfers between devices  5.15 us (2%)
    all_to_all x2, blocking collectives, expert_rows(): got = lax.all_to_all(send, 'exp', split_axis=0, concat_axis=0, tiled=True)  30.6 us
    all_gather x2, waiting for transfers between devices, expert_rows(): lax.all_gather(got, ('ctx', 'dp'))  26.7 us
    reduce_scatter x2, waiting for transfers between devices, summed_rows(): lax.psum_scatter(arrange_sums(full_term, ctx_count, dp_count, exp_count,...  26.6 us
    all_gather x2, blocking collectives, sum_over(): return jnp.sum(lax.all_gather(x, axes).astype(jnp.float32), axis=0)  21.1 us
    all_gather x1, blocking collectives, per_device(): lax.all_gather(jnp.concatenate([both, probs_flat.reshape(-1, both.shape[1...  14.3 us
    all_gather x1, blocking collectives, per_device(): lax.all_gather(jnp.concatenate([state_local, decay_row], axis=1).astype(j...  12.1 us
    all_gather x1, blocking collectives, per_device(): lax.all_gather(jnp.concatenate([carry_cot.astype(jnp.bfloat16)] + gain_ro...  11.7 us
    unnamed x134, local copies, waits for them, and re-layouts  10.8 us
  transfers between devices with their start and end apart: 5, of which 4 were waited for; matrix products, arithmetic and copies ran while one was open for 18% of the time, Pallas kernels for 0%

profile of v4, /device:TPU:0, one launch (start us, length us, event | category | flops | bytes accessed | tf_op | source)
XLA Modules:
  0.0 252.4 jit_solution(4070090745454456025)
XLA Ops:
  10.3 1.1 fusion.22
  11.4 16.5 %all_to_all.15 = bf16[4,80,512]{2,1,0:T(8,128)(2,1)} all-to-all(bf16[4,80,512]{2,1,0:T(8,128)(2,1)S(1)} %bitcast.342), channel_id=1, replica_groups=mesh['ctx'=4,'exp'=4,'dp'=2] {'exp'}, dimensions={0} | all-to-all | bytes 655360 | tf_op jit(solution)/shard_map/all_to_all | solution.py:97
  28.0 1.0 copy.256
  29.1 0.8 fusion.123
  31.0 12.1 %all_gather.40 = bf16[4,8,65,64]{2,3,1,0:T(8,128)(2,1)S(1)} all-gather(bf16[1,8,65,64]{2,3,1,0:T(8,128)(2,1)S(1)} %pad_maximum_fusion), channel_id=1, replica_groups=mesh['ctx'=4,'exp'=4,'dp'=2] {'ctx'}, dimensions={0}, use_global_device_ids=true | all-gather | bytes 332800 | tf_op jit(solution)/shard_map/all_gather | solution.py:153
  45.8 10.3 %all-gather.6 = f32[8,1,128]{2,1,0:T(1,128)S(1)} all-gather(f32[1,1,128]{2,1,0:T(1,128)S(1)} %bitcast.354), channel_id=2, replica_groups=mesh['ctx'=4,'exp'=4,'dp'=2] {'exp','dp'}, dimensions={0}, use_global_device_ids=true | all-gather | bytes 4608 | tf_op jit(solution)/shard_map/all_gather | solution.py:27
  56.9 14.1 %all_to_all.16 = bf16[4,80,512]{2,1,0:T(8,128)(2,1)} all-to-all(bf16[4,80,512]{2,1,0:T(8,128)(2,1)S(1)} %bitcast.343), channel_id=1, replica_groups=mesh['ctx'=4,'exp'=4,'dp'=2] {'exp'}, dimensions={0} | all-to-all | bytes 655360 | tf_op jit(solution)/shard_map/all_to_all | solution.py:97
  71.3 2.0 fusion.152
  73.3 26.7 %all-gather.14.cloned.1.call-done = bf16[32,80,512]{2,1,0:T(8,128)(2,1)} async-done(((bf16[4,80,512]{2,1,0:T(8,128)(2,1)}), bf16[32,80,512]{2,1,0:T(8,128)(2,1)}) %all-gather.14.cloned.1.call-update) | async-done | bytes 2621456 | tf_op jit(solution)/shard_map/all_gather | solution.py:98
  100.0 1.8 fusion.153
  102.3 6.3 %fusion.2 = f32[320,1024]{1,0:T(8,128)S(1)} fusion(bf16[320,4096]{1,0:T(8,128)(2,1)S(1)} %constant_dynamic-update-slice_fusion.8, bf16[1,4096,1024]{2,1,0:T(8,128)(2,1)} %param.20), kind=kOutput, calls=%fused_computation.2 | convolution fusion | flops 2684354560 | bytes 12320768 | tf_op jit(solution)/shard_map/dot_general | solution.py:182
  108.9 1.5 copy-done.17
  110.4 3.0 %fusion.10 = f32[320,1024]{1,0:T(8,128)S(1)} fusion(bf16[320,4096]{1,0:T(8,128)(2,1)S(1)} %constant_dynamic-update-slice_fusion, bf16[1,4096,1024]{2,1,0:T(8,128)(2,1)S(1)} %bitcast.365), kind=kOutput, calls=%fused_computation.10 | convolution fusion | flops 2684354560 | bytes 12320768 | tf_op jit(solution)/shard_map/dot_general | solution.py:186
  113.4 1.1 slice-done.3
  114.5 4.5 %multiply_convert_fusion = (bf16[320,1024]{1,0:T(8,128)(2,1)}, bf16[320,1024]{1,0:T(8,128)(2,1)S(1)}, bf16[320,1024]{1,0:T(8,128)(2,1)}) fusion(f32[320,1024]{1,0:T(8,128)S(1)} %fusion.2, f32[320,1024]{1,0:T(8,128)S(1)} %fusion.10, bf16[320,4096]{1,0:T(8,128)(2,1)S(1)} %constant_dynamic-update-slice_fusion.8, bf16[1,4096,1024]{2,1,0:T(8,128)(2,1)S(1)} %bitcast.363), kind=kOutput, calls=%fused_computation.18 | convolution fusion | flops 2689269760 | bytes 15597568 | tf_op jit(solution)/shard_map/dot_general | solution.py:183
  119.0 2.9 %fusion = f32[320,4096]{1,0:T(8,128)S(1)} fusion(bf16[320,1024]{1,0:T(8,128)(2,1)S(1)} %get-tuple-element.124, bf16[1,4096,1024]{2,1,0:T(8,128)(2,1)S(1)} %bitcast.361), kind=kOutput, calls=%fused_computation | convolution fusion | flops 2684354560 | bytes 14286848 | tf_op jit(solution)/shard_map/dot_general | solution.py:189
  121.9 4.3 %fusion.15 = bf16[320,4096]{1,0:T(8,128)(2,1)S(1)} fusion(f32[320,4096]{1,0:T(8,128)S(1)} %fusion, bf16[320,1024]{1,0:T(8,128)(2,1)} %get-tuple-element.125, bf16[1,4096,1024]{2,1,0:T(8,128)(2,1)S(1)} %bitcast.363), kind=kOutput, calls=%fused_computation.16 | convolution fusion | flops 2686976000 | bytes 16908288 | tf_op jit(solution)/shard_map/dot_general | solution.py:191
  126.5 1.5 copy-done.1
  128.3 6.5 %fusion.18 = bf16[320,4096]{1,0:T(8,128)(2,1)S(1)} fusion(bf16[320,1024]{1,0:T(8,128)(2,1)} %get-tuple-element.15, bf16[1,4096,1024]{2,1,0:T(8,128)(2,1)} %param.22), kind=kOutput, calls=%fused_computation.17 | convolution fusion | flops 2685665280 | bytes 11665408 | tf_op jit(solution)/shard_map/dot_general | solution.py:197
  135.0 1.5 copy-done.2
  137.5 10.2 %convert_bitcast_fusion = bf16[1,4096,1024]{2,1,0:T(8,128)(2,1)} fusion(bf16[320,4096]{1,0:T(8,128)(2,1)} %copy-done.17, bf16[320,1024]{1,0:T(8,128)(2,1)} %get-tuple-element.15), kind=kOutput, calls=%fused_computation.12 | convolution fusion | flops 2688548864 | bytes 11665408 | tf_op jit(solution)/shard_map/dot_general | solution.py:210
  147.7 6.8 %convert_bitcast_fusion.1 = bf16[1,4096,1024]{2,1,0:T(8,128)(2,1)} fusion(bf16[320,4096]{1,0:T(8,128)(2,1)S(1)} %copy-done.19, bf16[320,1024]{1,0:T(8,128)(2,1)S(1)} %copy-done.41), kind=kOutput, calls=%fused_computation.13 | convolution fusion | flops 2688548864 | bytes 11665408 | tf_op jit(solution)/shard_map/dot_general | solution.py:207
  154.5 17.3 %reduce-scatter.3.cloned.1.call-done = bf16[320,512]{1,0:T(8,128)(2,1)} async-done(((bf16[2560,512]{1,0:T(8,128)(2,1)}), bf16[320,512]{1,0:T(8,128)(2,1)}) %reduce-scatter.3.cloned.1.call-update) | async-done | bytes 327696 | tf_op jit(solution)/shard_map/reduce_scatter | solution.py:102
  171.8 4.6 %all-to-all-start.2 = ((bf16[4,80,512]{2,1,0:T(8,128)(2,1)}), bf16[4,80,512]{2,1,0:T(8,128)(2,1)S(1)}, u32[]{:S(2)}, u32[]{:S(2)}) async-start(bf16[4,80,512]{2,1,0:T(8,128)(2,1)} %bitcast.345), calls=%async_computation.3 | async-start | bytes 655360 | tf_op jit(solution)/shard_map/all_to_all | solution.py:112
  176.5 8.7 %convert_bitcast_fusion.2 = bf16[1,4096,1024]{2,1,0:T(8,128)(2,1)} fusion(bf16[320,4096]{1,0:T(8,128)(2,1)} %copy-done.18, bf16[320,1024]{1,0:T(8,128)(2,1)S(1)} %copy-done.43), kind=kOutput, calls=%fused_computation.14 | convolution fusion | flops 2688548864 | bytes 11665408 | tf_op jit(solution)/shard_map/dot_general | solution.py:204
  185.1 1.6 all-to-all-done.2
  187.1 10.8 %all-gather.7 = f32[8,1,128]{2,1,0:T(1,128)S(1)} all-gather(f32[1,1,128]{2,1,0:T(1,128)S(1)} %bitcast.359), channel_id=5, replica_groups=mesh['ctx'=4,'exp'=4,'dp'=2] {'exp','dp'}, dimensions={0}, use_global_device_ids=true | all-gather | bytes 4608 | tf_op jit(solution)/shard_map/all_gather | solution.py:27
  200.2 11.7 %all-gather.4 = bf16[32,66,64]{1,2,0:T(8,128)(2,1)S(1)} all-gather(bf16[8,66,64]{1,2,0:T(8,128)(2,1)S(1)} %pad_maximum_fusion.1), channel_id=6, replica_groups=mesh['ctx'=4,'exp'=4,'dp'=2] {'ctx'}, dimensions={0}, use_global_device_ids=true | all-gather | bytes 337920 | tf_op jit(solution)/shard_map/all_gather | solution.py:224
  212.5 9.3 %reduce-scatter.5.cloned.1.call-done = bf16[320,512]{1,0:T(8,128)(2,1)} async-done(((bf16[2560,512]{1,0:T(8,128)(2,1)}), bf16[320,512]{1,0:T(8,128)(2,1)}) %reduce-scatter.5.cloned.1.call-update) | async-done | bytes 327696 | tf_op jit(solution)/shard_map/reduce_scatter | solution.py:102
  223.5 0.9 fusion.54
  225.4 14.3 %all-gather.8 = bf16[8,130,128]{2,1,0:T(8,128)(2,1)S(1)} all-gather(bf16[1,130,128]{2,1,0:T(8,128)(2,1)S(1)} %copy.282), channel_id=7, replica_groups=mesh['ctx'=4,'exp'=4,'dp'=2] {'exp','dp'}, dimensions={0}, use_global_device_ids=true | all-gather | bytes 299520 | tf_op jit(solution)/shard_map/all_gather | solution.py:242
  244.5 0.8 convolution_add_fusion.2
  (218 shorter events, 21.1 us)
Async XLA Ops:
  7.2 23.0 %copy-start = (bf16[128,64]{0,1:T(8,128)(2,1)S(1)}, bf16[128,64]{0,1:T(8,128)(2,1)}, u32[]{:S(2)}) copy-start(bf16[128,64]{0,1:T(8,128)(2,1)} %param.14) | copy-start | bytes 49156
  7.2 36.7 %copy-start.8 = (bf16[128,64]{0,1:T(8,128)(2,1)S(1)}, bf16[128,64]{0,1:T(8,128)(2,1)}, u32[]{:S(2)}) copy-start(bf16[128,64]{0,1:T(8,128)(2,1)} %param.15) | copy-start | bytes 49156
  7.2 64.1 %all-gather.12.cloned.1.call-start = ((), (), s32[]{:S(2)}) async-start(), calls=%async_computation.7 | async-start | bytes 2949120 | tf_op jit(solution)/shard_map/all_gather | solution.py:98
  10.1 46.5 %copy-start.24 = (s32[128]{0:T(128)}, s32[128]{0:T(128)S(1)}, u32[]{:S(2)}) copy-start(s32[128]{0:T(128)S(1)} %get-tuple-element.150) | copy-start | bytes 1540
  10.1 46.5 %copy-start.26 = (s32[128]{0:T(128)}, s32[128]{0:T(128)S(1)}, u32[]{:S(2)}) copy-start(s32[128]{0:T(128)S(1)} %get-tuple-element.151) | copy-start | bytes 1540
  27.9 17.7 %copy-start.10 = (bf16[128,512]{1,0:T(8,128)(2,1)S(1)}, bf16[128,512]{1,0:T(8,128)(2,1)}, u32[]{:S(2)}) copy-start(bf16[128,512]{1,0:T(8,128)(2,1)} %param.12) | copy-start | bytes 393220
  28.0 28.7 %copy-start.28 = (f32[512]{0:T(512)S(1)}, f32[512]{0:T(512)}, u32[]{:S(2)}) copy-start(f32[512]{0:T(512)} %param.19) | copy-start | bytes 6148
  28.0 72.0 %all-gather.14.cloned.1.call-start = ((), (), s32[]{:S(2)}) async-start(), calls=%async_computation.8 | async-start | bytes 2949120 | tf_op jit(solution)/shard_map/all_gather | solution.py:98
  29.9 15.6 %copy-start.15 = (f32[128,8]{0,1:T(8,128)}, f32[128,8]{0,1:T(8,128)S(1)}, u32[]{:S(2)}) copy-start(f32[128,8]{0,1:T(8,128)S(1)} %fusion.123) | copy-start | bytes 12292
  30.2 15.2 %copy-start.20 = (f32[128,8]{0,1:T(8,128)}, f32[128,8]{0,1:T(8,128)S(1)}, u32[]{:S(2)}) copy-start(f32[128,8]{0,1:T(8,128)S(1)} %get-tuple-element.147) | copy-start | bytes 12292
  45.8 25.6 %copy-start.4 = (bf16[128,512]{1,0:T(8,128)(2,1)}, bf16[128,512]{1,0:T(8,128)(2,1)S(1)}, u32[]{:S(2)}) copy-start(bf16[128,512]{1,0:T(8,128)(2,1)S(1)} %get-tuple-element.122) | copy-start | bytes 393220
  56.6 14.7 %copy-start.36 = (f32[128]{0:T(128)}, f32[128]{0:T(128)S(1)}, u32[]{:S(2)}) copy-start(f32[128]{0:T(128)S(1)} %get-tuple-element.155) | copy-start | bytes 1540
  71.1 100.8 %reduce-scatter.3.cloned.1.call-start = ((), (), s32[]{:S(2)}) async-start(), calls=%async_computation.5 | async-start | bytes 2949120 | tf_op jit(solution)/shard_map/reduce_scatter | solution.py:102
  102.2 11.1 %copy-start.18 = (bf16[320,4096]{1,0:T(8,128)(2,1)}, bf16[320,4096]{1,0:T(8,128)(2,1)S(1)}, u32[]{:S(2)}) copy-start(bf16[320,4096]{1,0:T(8,128)(2,1)S(1)} %constant_dynamic-update-slice_fusion.8) | copy-start | bytes 7864324
  128.0 93.7 %reduce-scatter.5.cloned.1.call-start = ((), (), s32[]{:S(2)}) async-start(), calls=%async_computation.6 | async-start | bytes 2949120 | tf_op jit(solution)/shard_map/reduce_scatter | solution.py:102
  147.7 28.7 %copy-start.43 = (bf16[320,1024]{1,0:T(8,128)(2,1)S(1)}, bf16[320,1024]{1,0:T(8,128)(2,1)}, u32[]{:S(2)}) copy-start(bf16[320,1024]{1,0:T(8,128)(2,1)} %copy-done.42) | copy-start | bytes 1966084
  171.8 14.9 %all-to-all-start.2 = ((bf16[4,80,512]{2,1,0:T(8,128)(2,1)}), bf16[4,80,512]{2,1,0:T(8,128)(2,1)S(1)}, u32[]{:S(2)}, u32[]{:S(2)}) async-start(bf16[4,80,512]{2,1,0:T(8,128)(2,1)} %bitcast.345), calls=%async_computation.3 | async-start | bytes 655360 | tf_op jit(solution)/shard_map/all_to_all | solution.py:112
  176.4 10.3 %copy-start.25 = (s32[128]{0:T(128)S(1)}, s32[128]{0:T(128)}, u32[]{:S(2)}) copy-start(s32[128]{0:T(128)} %copy-done.24) | copy-start | bytes 1540
  176.5 21.6 %copy-start.6 = (bf16[128,512]{1,0:T(8,128)(2,1)S(1)}, bf16[128,512]{1,0:T(8,128)(2,1)}, u32[]{:S(2)}) copy-start(bf16[128,512]{1,0:T(8,128)(2,1)} %param.23) | copy-start | bytes 393220
  176.5 21.6 %copy-start.40 = (f32[128]{0:T(128)S(1)}, f32[128]{0:T(128)}, u32[]{:S(2)}) copy-start(f32[128]{0:T(128)} %get-tuple-element.154) | copy-start | bytes 1540
  185.1 14.4 %copy-start.9 = (bf16[128,64]{0,1:T(8,128)(2,1)S(1)}, bf16[128,64]{0,1:T(8,128)(2,1)}, u32[]{:S(2)}) copy-start(bf16[128,64]{0,1:T(8,128)(2,1)} %param.15) | copy-start | bytes 49156
  185.1 14.4 %copy-start.21 = (f32[128,8]{0,1:T(8,128)S(1)}, f32[128,8]{0,1:T(8,128)}, u32[]{:S(2)}) copy-start(f32[128,8]{0,1:T(8,128)} %copy-done.20) | copy-start | bytes 12292
  198.0 14.2 %copy-start.31 = (f32[8]{0:T(128)S(1)}, f32[8]{0:T(128)}, u32[]{:S(2)}) copy-start(f32[8]{0:T(128)} %copy-done.30) | copy-start | bytes 100
  198.1 14.2 %copy-start.33 = (f32[8]{0:T(128)S(1)}, f32[8]{0:T(128)}, u32[]{:S(2)}) copy-start(f32[8]{0:T(128)} %copy-done.32) | copy-start | bytes 100
  198.1 14.2 %copy-start.35 = (f32[8]{0:T(128)S(1)}, f32[8]{0:T(128)}, u32[]{:S(2)}) copy-start(f32[8]{0:T(128)} %get-tuple-element.113) | copy-start | bytes 100
  198.3 23.5 %copy-start.39 = (f32[8]{0:T(128)S(1)}, f32[8]{0:T(128)}, u32[]{:S(2)}) copy-start(f32[8]{0:T(128)} %copy-done.38) | copy-start | bytes 100
  198.3 23.8 %copy-start.12 = (f32[128,8]{0,1:T(8,128)S(1)}, f32[128,8]{0,1:T(8,128)}, u32[]{:S(2)}) copy-start(f32[128,8]{0,1:T(8,128)} %copy-done.11) | copy-start | bytes 12292
  211.9 11.6 %copy-start.14 = (f32[128,128]{1,0:T(8,128)S(1)}, f32[128,128]{1,0:T(8,128)}, u32[]{:S(2)}) copy-start(f32[128,128]{1,0:T(8,128)} %copy-done.13) | copy-start | bytes 196612
  211.9 11.6 %copy-start.16 = (f32[128,8]{0,1:T(8,128)S(1)}, f32[128,8]{0,1:T(8,128)}, u32[]{:S(2)}) copy-start(f32[128,8]{0,1:T(8,128)} %copy-done.15) | copy-start | bytes 12292
  211.9 11.6 %copy-start.23 = (pred[128,128]{1,0:T(8,128)(4,1)S(1)}, pred[128,128]{1,0:T(8,128)(4,1)}, u32[]{:S(2)}) copy-start(pred[128,128]{1,0:T(8,128)(4,1)} %copy-done.22) | copy-start | bytes 49156
  212.4 11.9 %copy-start.3 = (bf16[4,80,512]{2,1,0:T(8,128)(2,1)S(1)}, bf16[4,80,512]{2,1,0:T(8,128)(2,1)}, u32[]{:S(2)}) copy-start(bf16[4,80,512]{2,1,0:T(8,128)(2,1)} %all_to_all.15) | copy-start | bytes 983044
  224.4 20.9 %copy-start.34 = (f32[128,2]{0,1:T(2,128)S(1)}, f32[128,2]{0,1:T(2,128)}, u32[]{:S(2)}) copy-start(f32[128,2]{0,1:T(2,128)} %param.18) | copy-start | bytes 3076
  (23 other events, 122.0 us)
Sparse Core Ops, SparseCore 0:
  28.1 30.6 all-gather.11
  71.2 28.7 all-gather.13
  128.1 43.6 reduce-scatter.2
  175.0 46.6 reduce-scatter.4
